TPU v7x, 32 devices: a whole 2x2x4 slice. The times are simulated.
32 devices in a mesh: group: 2 (over x), circ: 8 (over z, y), axial: 2 (over core).
Axes of the slice: x: 2, y: 2, z: 4, core: 2. Of those that a mesh axis runs over, the one named last changes fastest.
Arguments:
- features: bfloat16 [3, 8, 64, 128], P(None, ('group', 'axial'), 'circ'), parts along dimension 1, may hold values from -6 to 6
- w_first: bfloat16 [27, 64, 3], replicated, may hold values from -0.625 to 0.625
- w_middle: bfloat16 [27, 64, 64], replicated, may hold values from -0.15625 to 0.15625
- w_last: bfloat16 [27, 4, 64], replicated, may hold values from -0.15625 to 0.15625
- diffusion: float32 [3, 8, 64, 128], P(None, ('group', 'axial'), 'circ'), parts along dimension 1, may hold values from 0.3 to 3
- pressure: float32 [3, 8, 64, 128], P(None, ('group', 'axial'), 'circ'), parts along dimension 1, may hold values from 0.5 to 2
- advection: float32 [3, 8, 64, 128], P(None, ('group', 'axial'), 'circ'), parts along dimension 1, may hold values from -3 to 3
- forcing: float32 [3, 8, 64, 128], P(None, ('group', 'axial'), 'circ'), parts along dimension 1, may hold values from -6 to 6
Outputs:
- predicted: bfloat16 [4, 8, 64, 128], P(None, ('group', 'axial'), 'circ'), parts along dimension 1
- grad_first: float32 [54, 64, 3], P('group'), parts along dimension 0
- grad_middle: float32 [54, 64, 64], P('group'), parts along dimension 0
- grad_last: float32 [54, 4, 64], P('group'), parts along dimension 0
There are 2 independent parts, one for each index of `group`. A program takes and returns all parts, laid end to end along the dimension named above; an argument that names none is the same for every part. Nothing has to cross between parts.
All inputs are finite; a program needn't handle non-finite values.
Results may differ from a plain program's by a relative error of at most 0.0056.
Values may be sent and summed in bfloat16 or wider, within the bound.
A program may use at most 64 MiB of HBM per device.

v0:
```python
import jax
import jax.numpy as jnp
from jax import lax
from jax.sharding import PartitionSpec as P


def with_halo(value, sides, width, wrap):
    for axis, dim in sides:
        count, length = (lax.axis_size(axis), value.shape[dim])
        up = [(i, (i + 1) % count) for i in range(count if wrap else count - 1)]
        down = [(j, i) for i, j in up]
        last = lax.slice_in_dim(value, length - width, length, axis=dim)
        leading = lax.slice_in_dim(value, 0, width, axis=dim)
        before = lax.ppermute(last, axis, up)
        after = lax.ppermute(leading, axis, down)
        value = jnp.concatenate([before, value, after], axis=dim)
    return value


def cycle_extend(field):
    return with_halo(field, (("circ", 2),), 1, True)


def slab_extend(field):
    return with_halo(field, (("axial", 1),), 1, False)


def extend(field):
    field = cycle_extend(slab_extend(field))
    return jnp.pad(field, ((0, 0), (0, 0), (0, 0), (1, 1)))


def cycle_return(padded):
    edges = jnp.concatenate([padded[:, :, :1], padded[:, :, -1:]], axis=2)
    arrived = with_halo(edges, (("circ", 2),), 1, True)
    inner = padded[:, :, 1:-1]
    inner = inner.at[:, :, :1].add(arrived[:, :, :1])
    inner = inner.at[:, :, -1:].add(arrived[:, :, -1:])
    return inner


def slab_return(padded):
    edges = jnp.concatenate([padded[:, :1], padded[:, -1:]], axis=1)
    arrived = with_halo(edges, (("axial", 1),), 1, False)
    inner = padded[:, 1:-1]
    inner = inner.at[:, :1].add(arrived[:, :1])
    inner = inner.at[:, -1:].add(arrived[:, -1:])
    return inner


def retract(padded):
    padded = padded[:, :, :, 1:-1]
    return slab_return(cycle_return(padded))


def window(padded, offset, flipped):
    first_off = offset // 9
    second_off = offset // 3 % 3
    third_off = offset % 3
    if flipped:
        first_off, second_off, third_off = (2 - first_off, 2 - second_off, 2 - third_off)
    rows = padded.shape[1] - 2
    cols = padded.shape[2] - 2
    depth = padded.shape[3] - 2
    return padded[
        :,
        first_off : first_off + rows,
        second_off : second_off + cols,
        third_off : third_off + depth,
    ]


def convolve(padded, weights):
    total = None
    for offset in range(27):
        term = jnp.einsum(
            "oi,iabr->oabr",
            weights[offset],
            window(padded, offset, False),
            preferred_element_type=jnp.float32,
        )
        total = term if total is None else total + term
    return total


def transposed(padded, weights):
    total = None
    for offset in range(27):
        term = jnp.einsum(
            "oi,oabr->iabr",
            weights[offset],
            window(padded, offset, True),
            preferred_element_type=jnp.float32,
        )
        total = term if total is None else total + term
    return total


def input_grad(cotangent, weights):
    return transposed(extend(cotangent), weights)


def weight_terms(cotangent, padded):
    terms = [
        jnp.einsum(
            "oabr,iabr->oi",
            cotangent,
            window(padded, offset, False),
            preferred_element_type=jnp.float32,
        )
        for offset in range(27)
    ]
    return jnp.stack(terms)


def residual_core(padded, diffusion, pressure, advection, forcing):
    centre = padded[:, 1:-1, 1:-1, 1:-1]
    ahead = (padded[:, 2:, 1:-1, 1:-1], padded[:, 1:-1, 2:, 1:-1], padded[:, 1:-1, 1:-1, 2:])
    behind = (padded[:, :-2, 1:-1, 1:-1], padded[:, 1:-1, :-2, 1:-1], padded[:, 1:-1, 1:-1, :-2])
    velocity = centre[:3]
    result = forcing
    for direction in range(3):
        result = result + diffusion[direction] * (
            ahead[direction][:3] - 2.0 * velocity + behind[direction][:3]
        )
        result = (
            result
            - advection[direction]
            * velocity[direction]
            * (ahead[direction][:3] - behind[direction][:3])
            * 0.5
        )
    slopes = jnp.stack([ahead[direction][3] - behind[direction][3] for direction in range(3)]) * 0.5
    return result - pressure * slopes


def body(features, w_first, w_middle, w_last, diffusion, pressure, advection, forcing):
    rows, cols, depth = (features.shape[1], features.shape[2], features.shape[3])
    cells = rows * cols * depth * lax.axis_size("circ") * lax.axis_size("axial")
    feat_pad = extend(features)
    first = jnp.tanh(convolve(feat_pad, w_first)).astype(jnp.bfloat16)
    first_pad = extend(first)
    middle = jnp.tanh(convolve(first_pad, w_middle)).astype(jnp.bfloat16)
    middle_pad = extend(middle)
    predicted = convolve(middle_pad, w_last).astype(jnp.bfloat16)
    field_pad = extend(predicted).astype(jnp.float32)

    def local_residual(field):
        return residual_core(field, diffusion, pressure, advection, forcing)

    resid, pullback = jax.vjp(local_residual, field_pad)
    (pad_grad,) = pullback(resid / (3.0 * cells))
    out_grad = retract(pad_grad).astype(jnp.bfloat16)
    grad_last = weight_terms(out_grad, middle_pad)
    middle_f = middle.astype(jnp.float32)
    middle_back = (input_grad(out_grad, w_last) * (1.0 - middle_f * middle_f)).astype(jnp.bfloat16)
    grad_middle = weight_terms(middle_back, first_pad)
    first_f = first.astype(jnp.float32)
    first_back = (input_grad(middle_back, w_middle) * (1.0 - first_f * first_f)).astype(
        jnp.bfloat16
    )
    grad_first = weight_terms(first_back, feat_pad)
    summed = lax.psum((grad_first, grad_middle, grad_last), ("circ", "axial"))
    return (predicted, summed[0], summed[1], summed[2])


def solution(mesh):
    placed = (
        P(None, ("group", "axial"), "circ", None),
        P(),
        P(),
        P(),
        P(None, ("group", "axial"), "circ", None),
        P(None, ("group", "axial"), "circ", None),
        P(None, ("group", "axial"), "circ", None),
        P(None, ("group", "axial"), "circ", None),
    )
    return jax.shard_map(
        body,
        mesh=mesh,
        in_specs=placed,
        out_specs=(
            P(None, ("group", "axial"), "circ", None),
            P("group", None, None),
            P("group", None, None),
            P("group", None, None),
        ),
        check_vma=False,
    )
```

profile of v0, /device:TPU:0, one launch (start us, length us, event | category | flops | bytes accessed | tf_op | source)
XLA Modules:
  0.0 225.2 jit_solution(14578821668438759444)
XLA Ops:
  7.9 2.3 %collective-permute-start = (bf16[3,1,8,128]{3,0,2,1:T(4,128)(2,1)S(1)}, bf16[3,1,8,128]{3,0,2,1:T(4,128)(2,1)S(1)}, u32[]{:S(2)}, u32[]{:S(2)}) collective-permute-start(bf16[3,1,8,128]{3,0,2,1:T(4,128)(2,1)S(1)} %copy.417), channel_id=1, source_target_pairs={{0,1},{2,3},{4,5},{6,7},{8,9},{10,11},{12,13},{14,15},{16,17},{18,... | collective-permute-start | bytes 18440 | tf_op jit(solution)/shard_map/ppermute | solution.py:14
  13.4 2.4 %collective-permute-start.2 = (bf16[3,4,1,128]{3,0,2,1:T(4,128)(2,1)S(1)}, bf16[3,4,1,128]{3,0,2,1:T(4,128)(2,1)S(1)}, u32[]{:S(2)}, u32[]{:S(2)}) collective-permute-start(bf16[3,4,1,128]{3,0,2,1:T(4,128)(2,1)S(1)} %get-tuple-element.125), channel_id=1, source_target_pairs={{0,2},{2,4},{4,6},{6,8},{8,10},{10,12},{12,14},{14,0},{1,3},{3,5},... | collective-permute-start | bytes 9224 | tf_op jit(solution)/shard_map/ppermute | solution.py:14
  15.8 3.1 %collective-permute-start.3 = (bf16[3,4,1,128]{3,0,2,1:T(4,128)(2,1)S(1)}, bf16[3,4,1,128]{3,0,2,1:T(4,128)(2,1)S(1)}, u32[]{:S(2)}, u32[]{:S(2)}) collective-permute-start(bf16[3,4,1,128]{3,0,2,1:T(4,128)(2,1)S(1)} %get-tuple-element.126), channel_id=1, source_target_pairs={{2,0},{4,2},{6,4},{8,6},{10,8},{12,10},{14,12},{0,14},{3,1},{5,3},... | collective-permute-start | bytes 9224 | tf_op jit(solution)/shard_map/ppermute | solution.py:15
  28.4 2.2 collective-permute-start.4
  32.1 1.7 collective-permute-done.5
  34.7 3.9 %collective-permute-start.7 = (bf16[64,4,1,128]{3,0,2,1:T(8,128)(2,1)S(1)}, bf16[64,4,1,128]{3,0,2,1:T(8,128)(2,1)S(1)}, u32[]{:S(2)}, u32[]{:S(2)}) collective-permute-start(bf16[64,4,1,128]{3,0,2,1:T(8,128)(2,1)S(1)} %get-tuple-element.86), channel_id=1, source_target_pairs={{2,0},{4,2},{6,4},{8,6},{10,8},{12,10},{14,12},{0,14},{3,1},{5,3},... | collective-permute-start | bytes 196616 | tf_op jit(solution)/shard_map/ppermute | solution.py:15
  39.1 1.9 collective-permute-done.6
  51.0 1.8 collective-permute-done.9
  52.9 4.8 %collective-permute-start.11 = (bf16[64,4,1,128]{3,0,2,1:T(8,128)(2,1)S(1)}, bf16[64,4,1,128]{3,0,2,1:T(8,128)(2,1)S(1)}, u32[]{:S(2)}, u32[]{:S(2)}) collective-permute-start(bf16[64,4,1,128]{3,0,2,1:T(8,128)(2,1)S(1)} %get-tuple-element.82), channel_id=1, source_target_pairs={{2,0},{4,2},{6,4},{8,6},{10,8},{12,10},{14,12},{0,14},{3,1},{5,3},... | collective-permute-start | bytes 196616 | tf_op jit(solution)/shard_map/ppermute | solution.py:15
  57.9 1.9 collective-permute-done.10
  68.0 1.7 collective-permute-done.13
  69.8 4.8 %collective-permute-start.15 = (bf16[4,4,1,128]{3,0,2,1:T(4,128)(2,1)S(1)}, bf16[4,4,1,128]{3,0,2,1:T(4,128)(2,1)S(1)}, u32[]{:S(2)}, u32[]{:S(2)}) collective-permute-start(bf16[4,4,1,128]{3,0,2,1:T(4,128)(2,1)S(1)} %get-tuple-element.124), channel_id=1, source_target_pairs={{2,0},{4,2},{6,4},{8,6},{10,8},{12,10},{14,12},{0,14},{3,1},{5,3},... | collective-permute-start | bytes 12296 | tf_op jit(solution)/shard_map/ppermute | solution.py:15
  77.6 4.8 %collective-permute-start.17 = (f32[4,4,1,128]{3,0,2,1:T(4,128)S(1)}, f32[4,4,1,128]{3,0,2,1:T(4,128)S(1)}, u32[]{:S(2)}, u32[]{:S(2)}) collective-permute-start(f32[4,4,1,128]{3,0,2,1:T(4,128)S(1)} %get-tuple-element.93), channel_id=1, source_target_pairs={{2,0},{4,2},{6,4},{8,6},{10,8},{12,10},{14,12},{0,14},{3,1},{5,3},... | collective-permute-start | bytes 24584 | tf_op jit(solution)/shard_map/ppermute | solution.py:15
  87.1 1.7 collective-permute-done.19
  89.0 2.1 collective-permute-start.20
  98.1 5.0 %collective-permute-start.23 = (bf16[4,4,1,128]{3,0,2,1:T(4,128)(2,1)S(1)}, bf16[4,4,1,128]{3,0,2,1:T(4,128)(2,1)S(1)}, u32[]{:S(2)}, u32[]{:S(2)}) collective-permute-start(bf16[4,4,1,128]{3,0,2,1:T(4,128)(2,1)S(1)} %get-tuple-element.104), channel_id=1, source_target_pairs={{2,0},{4,2},{6,4},{8,6},{10,8},{12,10},{14,12},{0,14},{3,1},{5,3},... | collective-permute-start | bytes 12296 | tf_op jit(solution)/shard_map/ppermute | solution.py:15
  104.5 5.0 %collective-permute-done.22 = bf16[4,4,1,128]{3,0,2,1:T(4,128)(2,1)S(1)} collective-permute-done((bf16[4,4,1,128]{3,0,2,1:T(4,128)(2,1)S(1)}, bf16[4,4,1,128]{3,0,2,1:T(4,128)(2,1)S(1)}, u32[]{:S(2)}, u32[]{:S(2)}) %collective-permute-start.22) | collective-permute-done | bytes 4128 | tf_op jit(solution)/shard_map/ppermute | solution.py:14
  124.7 1.6 collective-permute-start.24
  127.9 1.7 collective-permute-done.25
  132.2 2.1 collective-permute-done.27
  134.2 3.2 %collective-permute-done.26 = bf16[64,4,1,128]{3,0,2,1:T(8,128)(2,1)S(1)} collective-permute-done((bf16[64,4,1,128]{3,0,2,1:T(8,128)(2,1)S(1)}, bf16[64,4,1,128]{3,0,2,1:T(8,128)(2,1)S(1)}, u32[]{:S(2)}, u32[]{:S(2)}) %collective-permute-start.26) | collective-permute-done | bytes 65568 | tf_op jit(solution)/shard_map/ppermute | solution.py:14
  151.6 59.5 %all-reduce.32 = (f32[27,64,3]{1,2,0:T(4,128)S(1)}, f32[27,4,64]{2,1,0:T(4,128)}) all-reduce(f32[27,64,3]{1,2,0:T(4,128)S(1)} %fusion.192, f32[27,4,64]{2,1,0:T(4,128)S(1)} %fusion.165), channel_id=1, replica_groups=mesh['group'=2,'circ'=8,'axial'=2] {'circ','axial'}, use_global_device_ids=true, to_apply=%region_3.4 | all-reduce | flops 12096 | bytes 96768 | tf_op jit(solution)/shard_map/psum | solution.py:163
  211.7 4.6 %all-reduce.35.cloned.1.call-done = f32[27,64,64]{2,1,0:T(8,128)} async-done(((f32[27,64,64]{2,1,0:T(8,128)}), f32[27,64,64]{2,1,0:T(8,128)}) %all-reduce.35.cloned.1.call-update) | async-done | bytes 442384 | tf_op jit(solution)/shard_map/psum | solution.py:163
  216.2 2.2 copy.509
  (324 shorter events, 83.9 us)
Async XLA Ops:
  7.2 209.1 %all-reduce.35.cloned.1.call-start = ((), (), s32[]{:S(2)}) async-start(), calls=%async_computation | async-start | bytes 1769472 | tf_op jit(solution)/shard_map/psum | solution.py:163
  7.9 4.7 %collective-permute-start = (bf16[3,1,8,128]{3,0,2,1:T(4,128)(2,1)S(1)}, bf16[3,1,8,128]{3,0,2,1:T(4,128)(2,1)S(1)}, u32[]{:S(2)}, u32[]{:S(2)}) collective-permute-start(bf16[3,1,8,128]{3,0,2,1:T(4,128)(2,1)S(1)} %copy.417), channel_id=1, source_target_pairs={{0,1},{2,3},{4,5},{6,7},{8,9},{10,11},{12,13},{14,15},{16,17},{18,... | collective-permute-start | bytes 18440 | tf_op jit(solution)/shard_map/ppermute | solution.py:14
  13.4 7.0 %collective-permute-start.2 = (bf16[3,4,1,128]{3,0,2,1:T(4,128)(2,1)S(1)}, bf16[3,4,1,128]{3,0,2,1:T(4,128)(2,1)S(1)}, u32[]{:S(2)}, u32[]{:S(2)}) collective-permute-start(bf16[3,4,1,128]{3,0,2,1:T(4,128)(2,1)S(1)} %get-tuple-element.125), channel_id=1, source_target_pairs={{0,2},{2,4},{4,6},{6,8},{8,10},{10,12},{12,14},{14,0},{1,3},{3,5},... | collective-permute-start | bytes 9224 | tf_op jit(solution)/shard_map/ppermute | solution.py:14
  15.8 4.6 %collective-permute-start.3 = (bf16[3,4,1,128]{3,0,2,1:T(4,128)(2,1)S(1)}, bf16[3,4,1,128]{3,0,2,1:T(4,128)(2,1)S(1)}, u32[]{:S(2)}, u32[]{:S(2)}) collective-permute-start(bf16[3,4,1,128]{3,0,2,1:T(4,128)(2,1)S(1)} %get-tuple-element.126), channel_id=1, source_target_pairs={{2,0},{4,2},{6,4},{8,6},{10,8},{12,10},{14,12},{0,14},{3,1},{5,3},... | collective-permute-start | bytes 9224 | tf_op jit(solution)/shard_map/ppermute | solution.py:15
  28.4 3.7 %collective-permute-start.4 = (bf16[64,1,8,128]{3,0,2,1:T(8,128)(2,1)S(1)}, bf16[64,1,8,128]{3,0,2,1:T(8,128)(2,1)S(1)}, u32[]{:S(2)}, u32[]{:S(2)}) collective-permute-start(bf16[64,1,8,128]{3,0,2,1:T(8,128)(2,1)S(1)} %get-tuple-element.91), channel_id=1, source_target_pairs={{0,1},{2,3},{4,5},{6,7},{8,9},{10,11},{12,13},{14,15},{16,17},{18,... | collective-permute-start | bytes 393224 | tf_op jit(solution)/shard_map/ppermute | solution.py:14
  30.6 3.2 %collective-permute-start.5 = (bf16[64,1,8,128]{3,0,2,1:T(8,128)(2,1)S(1)}, bf16[64,1,8,128]{3,0,2,1:T(8,128)(2,1)S(1)}, u32[]{:S(2)}, u32[]{:S(2)}) collective-permute-start(bf16[64,1,8,128]{3,0,2,1:T(8,128)(2,1)S(1)} %get-tuple-element.92), channel_id=1, source_target_pairs={{1,0},{3,2},{5,4},{7,6},{9,8},{11,10},{13,12},{15,14},{17,16},{19,... | collective-permute-start | bytes 393224 | tf_op jit(solution)/shard_map/ppermute | solution.py:15
  33.9 7.1 %collective-permute-start.6 = (bf16[64,4,1,128]{3,0,2,1:T(8,128)(2,1)S(1)}, bf16[64,4,1,128]{3,0,2,1:T(8,128)(2,1)S(1)}, u32[]{:S(2)}, u32[]{:S(2)}) collective-permute-start(bf16[64,4,1,128]{3,0,2,1:T(8,128)(2,1)S(1)} %get-tuple-element.85), channel_id=1, source_target_pairs={{0,2},{2,4},{4,6},{6,8},{8,10},{10,12},{12,14},{14,0},{1,3},{3,5},... | collective-permute-start | bytes 196616 | tf_op jit(solution)/shard_map/ppermute | solution.py:14
  34.7 6.2 %collective-permute-start.7 = (bf16[64,4,1,128]{3,0,2,1:T(8,128)(2,1)S(1)}, bf16[64,4,1,128]{3,0,2,1:T(8,128)(2,1)S(1)}, u32[]{:S(2)}, u32[]{:S(2)}) collective-permute-start(bf16[64,4,1,128]{3,0,2,1:T(8,128)(2,1)S(1)} %get-tuple-element.86), channel_id=1, source_target_pairs={{2,0},{4,2},{6,4},{8,6},{10,8},{12,10},{14,12},{0,14},{3,1},{5,3},... | collective-permute-start | bytes 196616 | tf_op jit(solution)/shard_map/ppermute | solution.py:15
  49.5 3.2 %collective-permute-start.9 = (bf16[64,1,8,128]{3,0,2,1:T(8,128)(2,1)S(1)}, bf16[64,1,8,128]{3,0,2,1:T(8,128)(2,1)S(1)}, u32[]{:S(2)}, u32[]{:S(2)}) collective-permute-start(bf16[64,1,8,128]{3,0,2,1:T(8,128)(2,1)S(1)} %get-tuple-element.90), channel_id=1, source_target_pairs={{1,0},{3,2},{5,4},{7,6},{9,8},{11,10},{13,12},{15,14},{17,16},{19,... | collective-permute-start | bytes 393224 | tf_op jit(solution)/shard_map/ppermute | solution.py:15
  52.8 7.0 %collective-permute-start.10 = (bf16[64,4,1,128]{3,0,2,1:T(8,128)(2,1)S(1)}, bf16[64,4,1,128]{3,0,2,1:T(8,128)(2,1)S(1)}, u32[]{:S(2)}, u32[]{:S(2)}) collective-permute-start(bf16[64,4,1,128]{3,0,2,1:T(8,128)(2,1)S(1)} %get-tuple-element.81), channel_id=1, source_target_pairs={{0,2},{2,4},{4,6},{6,8},{8,10},{10,12},{12,14},{14,0},{1,3},{3,5},... | collective-permute-start | bytes 196616 | tf_op jit(solution)/shard_map/ppermute | solution.py:14
  52.9 7.0 %collective-permute-start.11 = (bf16[64,4,1,128]{3,0,2,1:T(8,128)(2,1)S(1)}, bf16[64,4,1,128]{3,0,2,1:T(8,128)(2,1)S(1)}, u32[]{:S(2)}, u32[]{:S(2)}) collective-permute-start(bf16[64,4,1,128]{3,0,2,1:T(8,128)(2,1)S(1)} %get-tuple-element.82), channel_id=1, source_target_pairs={{2,0},{4,2},{6,4},{8,6},{10,8},{12,10},{14,12},{0,14},{3,1},{5,3},... | collective-permute-start | bytes 196616 | tf_op jit(solution)/shard_map/ppermute | solution.py:15
  69.7 6.4 %collective-permute-start.14 = (bf16[4,4,1,128]{3,0,2,1:T(4,128)(2,1)S(1)}, bf16[4,4,1,128]{3,0,2,1:T(4,128)(2,1)S(1)}, u32[]{:S(2)}, u32[]{:S(2)}) collective-permute-start(bf16[4,4,1,128]{3,0,2,1:T(4,128)(2,1)S(1)} %get-tuple-element.123), channel_id=1, source_target_pairs={{0,2},{2,4},{4,6},{6,8},{8,10},{10,12},{12,14},{14,0},{1,3},{3,5},... | collective-permute-start | bytes 12296 | tf_op jit(solution)/shard_map/ppermute | solution.py:14
  69.8 6.4 %collective-permute-start.15 = (bf16[4,4,1,128]{3,0,2,1:T(4,128)(2,1)S(1)}, bf16[4,4,1,128]{3,0,2,1:T(4,128)(2,1)S(1)}, u32[]{:S(2)}, u32[]{:S(2)}) collective-permute-start(bf16[4,4,1,128]{3,0,2,1:T(4,128)(2,1)S(1)} %get-tuple-element.124), channel_id=1, source_target_pairs={{2,0},{4,2},{6,4},{8,6},{10,8},{12,10},{14,12},{0,14},{3,1},{5,3},... | collective-permute-start | bytes 12296 | tf_op jit(solution)/shard_map/ppermute | solution.py:15
  77.2 6.5 %collective-permute-start.16 = (f32[4,4,1,128]{3,0,2,1:T(4,128)S(1)}, f32[4,4,1,128]{3,0,2,1:T(4,128)S(1)}, u32[]{:S(2)}, u32[]{:S(2)}) collective-permute-start(f32[4,4,1,128]{3,0,2,1:T(4,128)S(1)} %get-tuple-element.94), channel_id=1, source_target_pairs={{0,2},{2,4},{4,6},{6,8},{8,10},{10,12},{12,14},{14,0},{1,3},{3,5},... | collective-permute-start | bytes 24584 | tf_op jit(solution)/shard_map/ppermute | solution.py:14
  77.6 6.2 %collective-permute-start.17 = (f32[4,4,1,128]{3,0,2,1:T(4,128)S(1)}, f32[4,4,1,128]{3,0,2,1:T(4,128)S(1)}, u32[]{:S(2)}, u32[]{:S(2)}) collective-permute-start(f32[4,4,1,128]{3,0,2,1:T(4,128)S(1)} %get-tuple-element.93), channel_id=1, source_target_pairs={{2,0},{4,2},{6,4},{8,6},{10,8},{12,10},{14,12},{0,14},{3,1},{5,3},... | collective-permute-start | bytes 24584 | tf_op jit(solution)/shard_map/ppermute | solution.py:15
  83.8 3.2 %collective-permute-start.18 = (f32[4,1,8,128]{3,0,2,1:T(4,128)S(1)}, f32[4,1,8,128]{3,0,2,1:T(4,128)S(1)}, u32[]{:S(2)}, u32[]{:S(2)}) collective-permute-start(f32[4,1,8,128]{3,0,2,1:T(4,128)S(1)} %get-tuple-element.102), channel_id=1, source_target_pairs={{0,1},{2,3},{4,5},{6,7},{8,9},{10,11},{12,13},{14,15},{16,17},{18,... | collective-permute-start | bytes 49160 | tf_op jit(solution)/shard_map/ppermute | solution.py:14
  89.0 9.1 %collective-permute-start.20 = (bf16[4,1,8,128]{3,0,2,1:T(4,128)(2,1)S(1)}, bf16[4,1,8,128]{3,0,2,1:T(4,128)(2,1)S(1)}, u32[]{:S(2)}, u32[]{:S(2)}) collective-permute-start(bf16[4,1,8,128]{3,0,2,1:T(4,128)(2,1)S(1)} %get-tuple-element.164), channel_id=1, source_target_pairs={{0,1},{2,3},{4,5},{6,7},{8,9},{10,11},{12,13},{14,15},{16,17},{18,... | collective-permute-start | bytes 24584 | tf_op jit(solution)/shard_map/ppermute | solution.py:14
  91.1 7.0 %collective-permute-start.21 = (bf16[4,1,8,128]{3,0,2,1:T(4,128)(2,1)S(1)}, bf16[4,1,8,128]{3,0,2,1:T(4,128)(2,1)S(1)}, u32[]{:S(2)}, u32[]{:S(2)}) collective-permute-start(bf16[4,1,8,128]{3,0,2,1:T(4,128)(2,1)S(1)} %get-tuple-element.165), channel_id=1, source_target_pairs={{1,0},{3,2},{5,4},{7,6},{9,8},{11,10},{13,12},{15,14},{17,16},{19,... | collective-permute-start | bytes 24584 | tf_op jit(solution)/shard_map/ppermute | solution.py:15
  98.1 6.4 %collective-permute-start.23 = (bf16[4,4,1,128]{3,0,2,1:T(4,128)(2,1)S(1)}, bf16[4,4,1,128]{3,0,2,1:T(4,128)(2,1)S(1)}, u32[]{:S(2)}, u32[]{:S(2)}) collective-permute-start(bf16[4,4,1,128]{3,0,2,1:T(4,128)(2,1)S(1)} %get-tuple-element.104), channel_id=1, source_target_pairs={{2,0},{4,2},{6,4},{8,6},{10,8},{12,10},{14,12},{0,14},{3,1},{5,3},... | collective-permute-start | bytes 12296 | tf_op jit(solution)/shard_map/ppermute | solution.py:15
  103.2 6.3 %collective-permute-start.22 = (bf16[4,4,1,128]{3,0,2,1:T(4,128)(2,1)S(1)}, bf16[4,4,1,128]{3,0,2,1:T(4,128)(2,1)S(1)}, u32[]{:S(2)}, u32[]{:S(2)}) collective-permute-start(bf16[4,4,1,128]{3,0,2,1:T(4,128)(2,1)S(1)} %get-tuple-element.103), channel_id=1, source_target_pairs={{0,2},{2,4},{4,6},{6,8},{8,10},{10,12},{12,14},{14,0},{1,3},{3,5},... | collective-permute-start | bytes 12296 | tf_op jit(solution)/shard_map/ppermute | solution.py:14
  124.7 3.2 %collective-permute-start.24 = (bf16[64,1,8,128]{3,0,2,1:T(8,128)(2,1)S(1)}, bf16[64,1,8,128]{3,0,2,1:T(8,128)(2,1)S(1)}, u32[]{:S(2)}, u32[]{:S(2)}) collective-permute-start(bf16[64,1,8,128]{3,0,2,1:T(8,128)(2,1)S(1)} %get-tuple-element.87), channel_id=1, source_target_pairs={{0,1},{2,3},{4,5},{6,7},{8,9},{10,11},{12,13},{14,15},{16,17},{18,... | collective-permute-start | bytes 393224 | tf_op jit(solution)/shard_map/ppermute | solution.py:14
  126.3 3.2 %collective-permute-start.25 = (bf16[64,1,8,128]{3,0,2,1:T(8,128)(2,1)S(1)}, bf16[64,1,8,128]{3,0,2,1:T(8,128)(2,1)S(1)}, u32[]{:S(2)}, u32[]{:S(2)}) collective-permute-start(bf16[64,1,8,128]{3,0,2,1:T(8,128)(2,1)S(1)} %get-tuple-element.88), channel_id=1, source_target_pairs={{1,0},{3,2},{5,4},{7,6},{9,8},{11,10},{13,12},{15,14},{17,16},{19,... | collective-permute-start | bytes 393224 | tf_op jit(solution)/shard_map/ppermute | solution.py:15
  129.5 4.7 %collective-permute-start.27 = (bf16[64,4,1,128]{3,0,2,1:T(8,128)(2,1)S(1)}, bf16[64,4,1,128]{3,0,2,1:T(8,128)(2,1)S(1)}, u32[]{:S(2)}, u32[]{:S(2)}) collective-permute-start(bf16[64,4,1,128]{3,0,2,1:T(8,128)(2,1)S(1)} %get-tuple-element.78), channel_id=1, source_target_pairs={{2,0},{4,2},{6,4},{8,6},{10,8},{12,10},{14,12},{0,14},{3,1},{5,3},... | collective-permute-start | bytes 196616 | tf_op jit(solution)/shard_map/ppermute | solution.py:15
  130.0 7.4 %collective-permute-start.26 = (bf16[64,4,1,128]{3,0,2,1:T(8,128)(2,1)S(1)}, bf16[64,4,1,128]{3,0,2,1:T(8,128)(2,1)S(1)}, u32[]{:S(2)}, u32[]{:S(2)}) collective-permute-start(bf16[64,4,1,128]{3,0,2,1:T(8,128)(2,1)S(1)} %get-tuple-element.77), channel_id=1, source_target_pairs={{0,2},{2,4},{4,6},{6,8},{8,10},{10,12},{12,14},{14,0},{1,3},{3,5},... | collective-permute-start | bytes 196616 | tf_op jit(solution)/shard_map/ppermute | solution.py:14
  (13 other events, 61.7 us)
Sparse Core Ops, SparseCore 0:
  124.8 91.3 all-reduce.34
where the time goes:
time: 226 us; the launch traced here: 225 us
  blocking collectives  59.5 us (26%)
  starting transfers between devices  53.3 us (24%)
  matrix products  53.1 us (23%)
  waiting for transfers between devices  31.6 us (14%)
  between operations  15.4 us (7%)
  local copies, waits for them, and re-layouts  8.15 us (4%)
  other arithmetic  4.19 us (2%)
    psum x1, blocking collectives, body(): summed = lax.psum((grad_first, grad_middle, grad_last), ('circ', 'axial'))  59.5 us
    ppermute x14, starting transfers between devices, with_halo(): after = lax.ppermute(leading, axis, down)  36 us
    dot_general x81, matrix products, convolve(): jnp.einsum('oi,iabr->oabr', weights[offset], window(padded, offset, False...  19.1 us
    dot_general x81, matrix products, weight_terms(): jnp.einsum('oabr,iabr->oi', cotangent, window(padded, offset, False), pre...  18 us
    ppermute x14, starting transfers between devices, with_halo(): before = lax.ppermute(last, axis, up)  17.3 us
    dot_general x54, matrix products, transposed(): jnp.einsum('oi,oabr->iabr', weights[offset], window(padded, offset, True)...  15.9 us
    ppermute x14, waiting for transfers between devices, with_halo(): before = lax.ppermute(last, axis, up)  15.2 us
    ppermute x14, waiting for transfers between devices, with_halo(): after = lax.ppermute(leading, axis, down)  11.9 us
  transfers between devices with their start and end apart: 29, of which 16 were waited for; matrix products, arithmetic and copies ran while one was open for 12% of the time, Pallas kernels for 0%

commit v1 on v0

v1 whole, which is shorter than its diff:
```python
import functools

import jax
import jax.numpy as jnp
from jax import lax
from jax.experimental import pallas as pl
from jax.experimental.pallas import tpu as pltpu
from jax.sharding import PartitionSpec as P

MESH = pl.DeviceIdType.MESH
F32 = jnp.float32
BF16 = jnp.bfloat16
HALO = 4


def dot(a, b):
    return jnp.dot(a, b, preferred_element_type=F32)


def dot_nt(a, b):
    return lax.dot_general(a, b, (((1,), (1,)), ((), ())), preferred_element_type=F32)


def from_behind(x):
    axis = x.ndim - 1
    lane = lax.broadcasted_iota(jnp.int32, x.shape, axis) % 128
    return jnp.where(lane == 0, 0.0, pltpu.roll(x, 1, axis))


def from_ahead(x):
    axis = x.ndim - 1
    lane = lax.broadcasted_iota(jnp.int32, x.shape, axis) % 128
    return jnp.where(lane == 127, 0.0, pltpu.roll(x, x.shape[axis] - 1, axis))


def shift_sum(z, rows):
    return from_behind(z[0:rows]) + z[rows : 2 * rows] + from_ahead(z[2 * rows : 3 * rows])


def shift_sum_back(z, rows):
    return from_ahead(z[0:rows]) + z[rows : 2 * rows] + from_behind(z[2 * rows : 3 * rows])


def ahead(x, d):
    if d == 0:
        return jnp.concatenate([x[1:], jnp.zeros_like(x[:1])], axis=0)
    if d == 1:
        return pltpu.roll(x, 15, 1)
    return from_ahead(x)


def behind(x, d):
    if d == 0:
        return jnp.concatenate([jnp.zeros_like(x[:1]), x[:-1]], axis=0)
    if d == 1:
        return pltpu.roll(x, 1, 1)
    return from_behind(x)


def low_half(x, y):
    sub = lax.broadcasted_iota(jnp.int32, x.shape, x.ndim - 2)
    return jnp.where(sub < 4, x, y)


def roll4(x):
    return pltpu.roll(x, 4, x.ndim - 2)


def pack_low(x0, x1):
    return low_half(x0, roll4(x1))


def pack_high(x0, x1):
    return low_half(roll4(x1), x0)


def halo_tiles(right, left):
    return low_half(right, left), roll4(low_half(left, right))


def kernel(n, cells, chunk, fchunk, *refs):
    (feat, wf, wb, w1, w3, w3t, diff, pres, adv, forc,
     pred_out, gfirst_out, gmid_out, glast_out,
     fc, fr, fl, mc, mr, ml, fsend, msend, fbase, fstage, fs, f1x, mid, m1x, pc, ph, psend,
     ogs, obase, og, mbx, fbs,
     red, redin, half, hin, gat, gfp, gfin, gfr,
     a_send, a_recv, p_send, p_recv, r_send, r_recv, s_send, s_recv, g_send, g_recv,
     x_send, x_recv, q_send, q_recv, h_send, h_recv) = refs
    c = lax.axis_index("circ")
    ax = lax.axis_index("axial")
    grp = lax.axis_index("group")
    sib = 1 - ax
    right = lax.rem(c + 1, n)
    left = lax.rem(c + n - 1, n)
    ndev = 2 * n
    me = c * 2 + ax

    def device(i):
        return (grp, i // 2, lax.rem(i, 2))

    def rcopy(src, dst, ss, rs, circ, axial):
        return pltpu.make_async_remote_copy(
            src_ref=src, dst_ref=dst, send_sem=ss, recv_sem=rs,
            device_id=(grp, circ, axial), device_id_type=MESH)

    barrier = pltpu.get_barrier_semaphore()

    def greet(j, carry):
        pl.semaphore_signal(barrier, inc=1, device_id=device(lax.rem(me + j, ndev)), device_id_type=MESH)
        return carry

    lax.fori_loop(1, ndev, greet, 0)

    x = feat[...].astype(F32)
    fc[ax] = x
    fsend[0] = pack_low(x[:, 0], x[:, 1])
    fsend[1] = pack_high(x[:, 0], x[:, 1])
    for g, ref in enumerate((diff, pres, adv, forc)):
        x = ref[...]
        mc[ax, 3 * g : 3 * g + 3] = x
        msend[0, 3 * g : 3 * g + 3] = pack_low(x[:, 0], x[:, 1])
        msend[1, 3 * g : 3 * g + 3] = pack_high(x[:, 0], x[:, 1])

    pl.semaphore_wait(barrier, ndev - 1)

    fcopies = []
    mcopies = []
    for out, cc, src_f, src_m, base in (
        (fcopies, fc, None, None, 0), (mcopies, mc, None, None, 5)):
        out.append(rcopy(cc.at[ax], cc.at[ax], a_send.at[base], a_recv.at[base], c, sib))
    for out, lo, hi, snd, base in ((fcopies, fr, fl, fsend, 0), (mcopies, mr, ml, msend, 5)):
        out.append(rcopy(snd.at[0], lo.at[ax], a_send.at[base + 1], a_recv.at[base + 1], left, ax))
        out.append(rcopy(snd.at[1], hi.at[ax], a_send.at[base + 2], a_recv.at[base + 2], right, ax))
        out.append(rcopy(snd.at[0], lo.at[ax], a_send.at[base + 3], a_recv.at[base + 3], left, sib))
        out.append(rcopy(snd.at[1], hi.at[ax], a_send.at[base + 4], a_recv.at[base + 4], right, sib))
    for cp in fcopies + mcopies:
        cp.start()

    for ref in (fs, f1x, m1x, og, mbx):
        ref[0] = jnp.zeros_like(ref[0])
        ref[5] = jnp.zeros_like(ref[5])
    fstage[...] = jnp.zeros_like(fstage)
    red[944:1024] = jnp.zeros((80, 128), BF16)
    gfp[...] = jnp.zeros_like(gfp)
    fbase[...] = jnp.zeros_like(fbase)
    obase[...] = jnp.zeros_like(obase)

    for cp in fcopies:
        cp.wait()

    for a in range(4):
        slab, l = a // 2, a % 2
        for ch in range(3):
            for j in range(14):
                b = j - 3
                if b < 0:
                    row = (8 + b) - 4 + (4 if l == 0 else 0)
                    v = fl[slab, ch, row : row + 1, :]
                elif b > 7:
                    row = (b - 8) + 4 * l
                    v = fr[slab, ch, row : row + 1, :]
                else:
                    v = fc[slab, ch, l, b : b + 1, :]
                fbase[a, ch : ch + 1, j * 128 : (j + 1) * 128] = v
        base = fbase[a]
        fstage[0:3, :] = from_behind(base)[0:3]
        fstage[3:6, :] = base[0:3]
        fstage[6:9, :] = from_ahead(base)[0:3]
        fs[a + 1] = fstage[...].astype(BF16)

    for a in range(4):
        xs = jnp.concatenate(
            [fs[a + da, :, db * 128 : db * 128 + 1536] for da in range(3) for db in range(3)], axis=0)
        first = jnp.tanh(dot(w1[...], xs)).astype(BF16)
        for db in range(3):
            f1x[a + 1, db * 64 : db * 64 + 64, :] = first[:, db * 128 : db * 128 + 1280]

    for a in range(4):
        for t in range(5):
            acc = None
            for da in range(3):
                if 0 <= a + da - 1 < 4:
                    term = dot(wf[da], f1x[a + da, :, t * 256 : t * 256 + 256])
                    acc = term if acc is None else acc + term
            mid[a, :, t * 256 : t * 256 + 256] = jnp.tanh(shift_sum(acc, 64)).astype(BF16)
        for db in range(3):
            m1x[a + 1, db * 64 : db * 64 + 64, :] = mid[a, :, db * 128 : db * 128 + 1024]

    for a in range(4):
        acc = None
        for da in range(3):
            if 0 <= a + da - 1 < 4:
                term = dot(w3[da], m1x[a + da])
                acc = term if acc is None else acc + term
        y = shift_sum(acc, 8).astype(BF16).astype(F32)
        for ch in range(4):
            for b in range(8):
                pc[ch, a, b : b + 1, :] = y[ch : ch + 1, b * 128 : b * 128 + 128]
    q = pc[...]
    for s in range(2):
        psend[0, :, s] = pack_low(q[:, 2 * s], q[:, 2 * s + 1])
        psend[1, :, s] = pack_high(q[:, 2 * s], q[:, 2 * s + 1])
    pcopies = [
        rcopy(psend.at[0], ph.at[0], p_send.at[0], p_recv.at[0], left, ax),
        rcopy(psend.at[1], ph.at[1], p_send.at[1], p_recv.at[1], right, ax),
    ]
    for cp in pcopies:
        cp.start()
    pred_out[...] = pc[:, pl.ds(2 * ax, 2)].astype(BF16)
    for cp in mcopies:
        cp.wait()
    for cp in pcopies:
        cp.wait()

    def metric(index):
        layers = []
        for slab in range(2):
            h = halo_tiles(mr[slab, index], ml[slab, index])
            for l in range(2):
                layers.append(jnp.concatenate([mc[slab, index, l], h[l]], axis=0))
        return jnp.stack(layers)

    field = []
    for ch in range(4):
        layers = []
        for s in range(2):
            h = halo_tiles(ph[0, ch, s], ph[1, ch, s])
            for l in range(2):
                layers.append(jnp.concatenate([pc[ch, 2 * s + l], h[l]], axis=0))
        field.append(jnp.stack(layers))
    D = [metric(d) for d in range(3)]
    A = [metric(6 + d) for d in range(3)]
    resid = [metric(9 + m) for m in range(3)]
    pm = [metric(3 + m) for m in range(3)]
    diffs = {}
    for m in range(3):
        for d in range(3):
            pa, pb = ahead(field[m], d), behind(field[m], d)
            diffs[m, d] = (pa - pb) * 0.5
            resid[m] = resid[m] + D[d] * (pa - 2.0 * field[m] + pb) - A[d] * field[d] * diffs[m, d]
        resid[m] = resid[m] - pm[m] * (ahead(field[3], m) - behind(field[3], m)) * 0.5
    t = [r / (3.0 * cells) for r in resid]
    out_p = None
    for m in range(3):
        total = None
        for d in range(3):
            dt = D[d] * t[m]
            y = A[d] * field[d] * t[m] * 0.5
            term = ahead(dt + y, d) + behind(dt - y, d) - 2.0 * dt
            total = term if total is None else total + term
        total = total - A[m] * (t[0] * diffs[0, m] + t[1] * diffs[1, m] + t[2] * diffs[2, m])
        ogs[m] = total
        y = pm[m] * t[m] * 0.5
        term = ahead(y, m) - behind(y, m)
        out_p = term if out_p is None else out_p + term
    ogs[3] = out_p

    fstage[0:16, :] = jnp.zeros((16, 1792), F32)
    for a in range(4):
        for ch in range(4):
            for j in range(12):
                b = (j - 2) % 16
                obase[a, ch : ch + 1, j * 128 : (j + 1) * 128] = ogs[ch, a, b : b + 1, :]
        base = obase[a]
        fstage[0:4, 0:1536] = from_ahead(base)[0:4]
        fstage[4:8, 0:1536] = base[0:4]
        fstage[8:12, 0:1536] = from_behind(base)[0:4]
        og[a + 1] = fstage[:, 0:1536].astype(BF16)

    for a in range(4):
        xs = jnp.concatenate(
            [og[a + 2 - da, :, (2 - db) * 128 : (2 - db) * 128 + 1280] for da in range(3) for db in range(3)],
            axis=0)
        mf = mid[a].astype(F32)
        back = (dot(w3t[...], xs) * (1.0 - mf * mf)).astype(BF16)
        for db in range(3):
            mbx[a + 1, db * 64 : db * 64 + 64, :] = back[:, (2 - db) * 128 : (2 - db) * 128 + 1024]

    own = 2 * ax + 1
    gm = [None] * 3
    gl = [None] * 3
    for l in range(2):
        m = mbx[own + l, 64:128, :].astype(F32)
        mbs = jnp.concatenate([from_ahead(m), m, from_behind(m)], axis=0).astype(BF16)
        ogo = og[own + l, :, 256:1280]
        for da in range(3):
            term = dot_nt(mbs, f1x[own + l + da - 1, :, 128:1152])
            gm[da] = term if gm[da] is None else gm[da] + term
            term = dot_nt(ogo, m1x[own + l + da - 1])
            gl[da] = term if gl[da] is None else gl[da] + term

    def block(parts, dd):
        return parts[dd // 3][:, dd % 3 * 64 : dd % 3 * 64 + 64]

    for p in range(4):
        red[p * 192 : p * 192 + 192] = jnp.concatenate(
            [block(gm, 2 * p), block(gm, 2 * p + 1)], axis=1).astype(BF16)
        red[864 + p * 16 : 880 + p * 16] = jnp.concatenate(
            [block(gl, 2 * p), block(gl, 2 * p + 1)], axis=1).astype(BF16)
    lastm, lastl = block(gm, 8), block(gl, 8)
    red[768:864] = jnp.concatenate([lastm[0:96], lastm[96:192]], axis=1).astype(BF16)
    red[928:944] = jnp.concatenate([lastl, jnp.zeros_like(lastl)], axis=1).astype(BF16)

    hrows = red.shape[0] // 2
    swap = rcopy(red.at[pl.ds(pl.multiple_of(sib * hrows, 16), hrows)], redin, r_send, r_recv, c, sib)
    swap.start()

    def first_back(l):
        acc = None
        for da in range(3):
            term = dot(wb[da], mbx[own + l + 1 - da])
            acc = term if acc is None else acc + term
        ff = f1x[own + l, 64:128, 128:1152].astype(F32)
        return (shift_sum_back(acc, 64) * (1.0 - ff * ff)).astype(BF16)

    fbs[0] = first_back(0)
    swap.wait()
    half[...] = (red[pl.ds(pl.multiple_of(ax * hrows, 16), hrows)].astype(F32) + redin[...].astype(F32)).astype(BF16)

    def scatter(j):
        peer = lax.rem(c + j, n)
        return rcopy(half.at[pl.ds(pl.multiple_of(peer * chunk, 16), chunk)], hin.at[j],
                     s_send.at[j], s_recv.at[j], peer, ax)

    def start_scatter(j, carry):
        scatter(j).start()
        return carry

    lax.fori_loop(1, n, start_scatter, 0)

    fbs[1] = first_back(1)
    gf = None
    for l in range(2):
        xs = jnp.concatenate(
            [fs[own + l + da - 1, :, (2 + db) * 128 : (2 + db) * 128 + 1024]
             for da in range(3) for db in range(3)], axis=0)
        term = dot_nt(fbs[l], xs)
        gf = term if gf is None else gf + term
    gfp[0:64, :] = gf[:, 0:128]
    gfp[64:128, 0:16] = gf[:, 128:144]

    def fscatter(j):
        peer = lax.rem(me + j, ndev)
        return pltpu.make_async_remote_copy(
            src_ref=gfp.at[pl.ds(pl.multiple_of(peer * fchunk, 8), fchunk)], dst_ref=gfin.at[j],
            send_sem=x_send.at[j], recv_sem=x_recv.at[j], device_id=device(peer), device_id_type=MESH)

    def start_fscatter(j, carry):
        fscatter(j).start()
        return carry

    lax.fori_loop(1, ndev, start_fscatter, 0)

    def add_chunk(j, total):
        scatter(j).wait()
        return total + hin[j].astype(F32)

    mine = half[pl.ds(pl.multiple_of(c * chunk, 16), chunk)].astype(F32)
    total = lax.fori_loop(1, n, add_chunk, mine)
    here = pl.multiple_of(c * chunk, 16)
    gat[ax, pl.ds(here, chunk)] = total.astype(BF16)

    def gather(j):
        part = gat.at[ax, pl.ds(here, chunk)]
        return rcopy(part, part, g_send.at[j], g_recv.at[j], lax.rem(c + j, n), ax)

    def start_gather(j, carry):
        gather(j).start()
        return carry

    lax.fori_loop(1, n, start_gather, 0)

    def forward(j):
        origin = lax.rem(c + n - j, n)
        part = gat.at[ax, pl.ds(pl.multiple_of(origin * chunk, 16), chunk)]
        return rcopy(part, part, h_send.at[j], h_recv.at[j], c, sib)

    forward(0).start()

    def fadd(j, total):
        fscatter(j).wait()
        return total + gfin[j]

    fmine = gfp[pl.ds(pl.multiple_of(me * fchunk, 8), fchunk)]
    fhere = pl.multiple_of(me * fchunk, 8)
    gfr[pl.ds(fhere, fchunk)] = lax.fori_loop(1, ndev, fadd, fmine)

    def fgather(j):
        peer = lax.rem(me + j, ndev)
        part = gfr.at[pl.ds(fhere, fchunk)]
        return pltpu.make_async_remote_copy(
            src_ref=part, dst_ref=part, send_sem=q_send.at[j], recv_sem=q_recv.at[j],
            device_id=device(peer), device_id_type=MESH)

    def start_fgather(j, carry):
        fgather(j).start()
        return carry

    lax.fori_loop(1, ndev, start_fgather, 0)

    def relay(j, carry):
        gather(j).wait()
        forward(j).start()
        return carry

    lax.fori_loop(1, n, relay, 0)

    def end_forward(j, carry):
        forward(j).wait()
        return carry

    lax.fori_loop(0, n, end_forward, 0)

    def rows_of(start, count, lanes):
        hr = hrows
        if start + count <= hr:
            return gat[0, start : start + count, lanes : lanes + 64]
        if start >= hr:
            return gat[1, start - hr : start - hr + count, lanes : lanes + 64]
        return jnp.concatenate(
            [gat[0, start:hr, lanes : lanes + 64], gat[1, 0 : start + count - hr, lanes : lanes + 64]], axis=0)

    for dd in range(9):
        if dd < 8:
            lblock = rows_of(864 + dd // 2 * 16, 16, dd % 2 * 64).astype(F32)
        else:
            lblock = rows_of(928, 16, 0).astype(F32)
        for dr in range(3):
            k = dd * 3 + dr
            glast_out[k] = lblock[dr * 4 : dr * 4 + 4]
            if dd < 8:
                gmid_out[k] = rows_of(dd // 2 * 192 + dr * 64, 64, dd % 2 * 64).astype(F32)
            elif dr == 0:
                gmid_out[k] = rows_of(768, 64, 0).astype(F32)
            elif dr == 1:
                gmid_out[k, 0:32] = rows_of(832, 32, 0).astype(F32)
                gmid_out[k, 32:64] = rows_of(768, 32, 64).astype(F32)
            else:
                gmid_out[k] = rows_of(800, 64, 64).astype(F32)

    def end_fgather(j, carry):
        fgather(j).wait()
        return carry

    lax.fori_loop(1, ndev, end_fgather, 0)
    g0 = gfr[0:64, :]
    g1 = gfr[64:128, :]
    for dd in range(9):
        src = g0 if dd < 8 else g1
        for dr in range(3):
            start = (dd * 16) % 128 + dr * 3
            gfirst_out[dd * 3 + dr] = src[:, start : start + 3]


def body(features, w_first, w_middle, w_last, diffusion, pressure, advection, forcing):
    n = lax.axis_size("circ")
    ndev = 2 * n
    rows, cols, depth = features.shape[1:]
    cells = rows * cols * depth * ndev
    chunk = max(16, 512 // n)
    rrows = chunk * n * 2
    fchunk = max(8, 128 // ndev)
    frows = fchunk * ndev

    w = w_middle.reshape(3, 3, 3, 64, 64)
    wf = w.transpose(0, 2, 3, 1, 4).reshape(3, 192, 192)
    wb = w.transpose(0, 2, 4, 1, 3).reshape(3, 192, 192)
    w1 = w_first.reshape(3, 3, 3, 64, 3).transpose(3, 0, 1, 2, 4).reshape(64, 9, 9)
    w1 = jnp.pad(w1, ((0, 0), (0, 0), (0, 7))).reshape(64, 144)
    wl = w_last.reshape(3, 3, 3, 4, 64)
    w3 = jnp.pad(wl.transpose(0, 2, 3, 1, 4), ((0, 0), (0, 0), (0, 4), (0, 0), (0, 0))).reshape(3, 24, 192)
    w3 = jnp.pad(w3, ((0, 0), (0, 8), (0, 0)))
    w3t = wl.transpose(4, 0, 1, 2, 3).reshape(64, 9, 12)
    w3t = jnp.pad(w3t, ((0, 0), (0, 0), (0, 4))).reshape(64, 144)

    V = pltpu.VMEM
    dma = pltpu.SemaphoreType.DMA
    scratch = [
        V((2, 3, 2, 8, 128), F32), V((2, 3, 8, 128), F32), V((2, 3, 8, 128), F32),
        V((2, 12, 2, 8, 128), F32), V((2, 12, 8, 128), F32), V((2, 12, 8, 128), F32),
        V((2, 3, 8, 128), F32), V((2, 12, 8, 128), F32),
        V((4, 8, 1792), F32), V((16, 1792), F32), V((6, 16, 1792), BF16),
        V((6, 192, 1280), BF16), V((4, 64, 1280), BF16), V((6, 192, 1024), BF16),
        V((4, 4, 8, 128), F32), V((2, 4, 2, 8, 128), F32), V((2, 4, 2, 8, 128), F32),
        V((4, 4, 16, 128), F32), V((4, 8, 1536), F32), V((6, 16, 1536), BF16),
        V((6, 192, 1024), BF16), V((2, 64, 1024), BF16),
        V((rrows, 128), BF16), V((rrows // 2, 128), BF16), V((rrows // 2, 128), BF16),
        V((n, chunk, 128), BF16), V((2, rrows // 2, 128), BF16),
        V((frows, 128), F32), V((ndev, fchunk, 128), F32), V((frows, 128), F32),
        dma((10,)), dma((10,)), dma((2,)), dma((2,)), dma, dma, dma((n,)), dma((n,)), dma((n,)), dma((n,)),
        dma((ndev,)), dma((ndev,)), dma((ndev,)), dma((ndev,)), dma((n,)), dma((n,)),
    ]
    vm = pl.BlockSpec(memory_space=pltpu.VMEM)
    return pl.pallas_call(
        functools.partial(kernel, n, cells, chunk, fchunk),
        out_shape=(
            jax.ShapeDtypeStruct((4, rows, cols, depth), BF16),
            jax.ShapeDtypeStruct((27, 64, 3), F32),
            jax.ShapeDtypeStruct((27, 64, 64), F32),
            jax.ShapeDtypeStruct((27, 4, 64), F32),
        ),
        in_specs=[vm] * 10,
        out_specs=(vm,) * 4,
        scratch_shapes=scratch,
        compiler_params=pltpu.CompilerParams(
            collective_id=0, has_side_effects=True, vmem_limit_bytes=48 * 1024 * 1024),
    )(features, wf, wb, w1, w3, w3t, diffusion, pressure, advection, forcing)


def solution(mesh):
    field = P(None, ("group", "axial"), "circ", None)
    grad = P("group", None, None)
    return jax.shard_map(
        body,
        mesh=mesh,
        in_specs=(field, P(), P(), P(), field, field, field, field),
        out_specs=(field, grad, grad, grad),
        check_vma=False,
    )
```

time: 226 us -> 43.8 us (0.19)
  blocking collectives: 59.5 us -> 0 us
  starting transfers between devices: 53.3 us -> 0 us
  matrix products: 53.1 us -> 0 us
  Pallas kernels: 0 us -> 34.5 us
  waiting for transfers between devices: 31.6 us -> 0 us
  between operations: 15.4 us -> 0.77 us
  other arithmetic: 4.19 us -> 0 us
    psum x1 -> x0, blocking collectives: 59.5 us -> none  [body(): summed = lax.psum((grad_first, grad_middle, grad_last), ('circ', 'axial'))]
    ppermute x28 -> x0, starting transfers between devices: 53.3 us -> none  [the longest x14 36 us: with_halo(): after = lax.ppermute(leading, axis, down)]
    dot_general x216 -> x0, matrix products: 53.1 us -> none  [the longest x81 19.1 us: convolve(): jnp.einsum('oi,iabr->oabr', weights[offset], window(padded, offset, False...]
    pallas_call x0 -> x1, Pallas kernels: none -> 34.5 us  [body(): pl.pallas_call(functools.partial(kernel, n, cells, chunk, fchunk), out_sh...]
    ppermute x28 -> x0, waiting for transfers between devices: 27.1 us -> none  [the longest x14 15.2 us: with_halo(): before = lax.ppermute(last, axis, up)]
    psum x1 -> x0, waiting for transfers between devices: 4.56 us -> none  [body(): summed = lax.psum((grad_first, grad_middle, grad_last), ('circ', 'axial'))]
    reshape x0 -> x10, local copies, waits for them, and re-layouts: none -> 3.95 us  [the longest x2 1.35 us: body(): w = w_middle.reshape(3, 3, 3, 64, 64)]
    slice x13 -> x0, local copies, waits for them, and re-layouts: 2.9 us -> none  [the longest x2 2 us: convolve(): weights[offset]]
  transfers between devices with their start and end apart: 29 -> 0, of which waited for: 16 -> 0; matrix products, arithmetic and copies ran while one was open for 12% -> 0% of each run, Pallas kernels for 0% -> 0%
where the time goes in v1:
time: 43.8 us; the launch traced here: 43.5 us
  Pallas kernels  34.5 us (79%)
  local copies, waits for them, and re-layouts  8.22 us (19%)
  between operations  0.77 us (2%)
    pallas_call x1, Pallas kernels, body(): pl.pallas_call(functools.partial(kernel, n, cells, chunk, fchunk), out_sh...  34.5 us
    unnamed x18, local copies, waits for them, and re-layouts  3.2 us
    reshape x2, local copies, waits for them, and re-layouts, body(): w = w_middle.reshape(3, 3, 3, 64, 64)  1.35 us
    pallas_call x1, local copies, waits for them, and re-layouts, body(): pl.pallas_call(functools.partial(kernel, n, cells, chunk, fchunk), out_sh...  0.99 us

profile of v1, /device:TPU:0, one launch (start us, length us, event | category | flops | bytes accessed | tf_op | source)
XLA Modules:
  0.0 43.5 jit_solution(13825892507987599289)
XLA Ops:
  0.6 0.8 %copy.25 = bf16[27,64,3]{1,2,0:T(4,128)(2,1)S(1)} copy(bf16[27,64,3]{1,0,2:T(8,128)(2,1)} %param.9) | data formatting | bytes 20736 | tf_op jit(solution)/shard_map/reshape | solution.py:468
  1.5 0.1 copy.22.refs_3_
  1.6 0.8 %reshape.46 = bf16[64,9,12]{0,2,1:T(8,128)(2,1)S(1)} reshape(bf16[64,3,3,3,4]{0,4,3,2,1:T(4,128)(2,1)} %bitcast.26) | data formatting | bytes 27648 | tf_op jit(solution)/shard_map/reshape | solution.py:473
  2.4 0.0 copy-start.6
  2.4 0.1 copy.23.refs_5_
  2.5 0.6 %copy-done.6 = bf16[27,4,64]{2,1,0:T(4,128)(2,1)S(1)} copy-done((bf16[27,4,64]{2,1,0:T(4,128)(2,1)S(1)}, bf16[27,4,64]{2,1,0:T(4,128)(2,1)}, u32[]{:S(2)}) %copy-start.6) | copy-done | bytes 13848
  3.2 0.1 reshape.45
  3.3 1.0 %copy.19 = bf16[3,3,3,64,64]{3,1,4,2,0:T(4,128)(2,1)S(1)} copy(bf16[3,3,3,64,64]{4,3,2,1,0:T(8,128)(2,1)S(1)} %bitcast.21) | data formatting | bytes 442368 | tf_op jit(solution)/shard_map/reshape | solution.py:465
  4.3 0.4 reshape.40.refs_2_
  4.7 0.4 copy.28
  5.1 0.0 copy-start
  5.1 0.0 copy-start.1
  5.1 0.0 copy-start.2
  5.1 0.0 copy-start.4
  5.1 0.4 reshape.39.refs_1_
  5.5 0.3 copy-done
  5.8 0.0 copy-done.1
  5.8 0.0 copy-done.2
  5.8 0.0 copy-done.3
  5.9 34.5 %shard_map.111 = (bf16[4,2,8,128]{3,2,1,0:T(8,128)(2,1)S(1)}, f32[27,64,3]{2,1,0:T(8,128)S(1)}, f32[27,64,64]{2,1,0:T(8,128)S(1)}, f32[27,4,64]{2,1,0:T(4,128)S(1)}) custom-call(bf16[3,2,8,128]{3,2,1,0:T(8,128)(2,1)S(1)} %copy-done.4, bf16[3,192,192]{2,1,0:T(8,128)(2,1)S(1)} %reshape.39.refs_1_, bf16[3,192,192]{2,1,0:T(8,128)(2,1)S(1)} %reshape.40.refs_2_, ...), custom_call_target="tpu_custom_call" | custom-call | tf_op jit(solution)/shard_map/pallas_call | solution.py:494
  40.4 1.0 %copy.24 = f32[27,64,3]{1,0,2:T(8,128)} copy(f32[27,64,3]{2,1,0:T(8,128)S(1)} %get-tuple-element.9) | data formatting | bytes 41472 | tf_op jit(solution)/shard_map/pallas_call | solution.py:494
  41.4 0.6 %copy.32 = bf16[4,2,8,128]{3,2,1,0:T(8,128)(2,1)} copy(bf16[4,2,8,128]{3,2,1,0:T(8,128)(2,1)S(1)} %get-tuple-element.16) | data formatting | bytes 32768
  42.0 0.9 %copy.33 = f32[27,64,64]{2,1,0:T(8,128)} copy(f32[27,64,64]{2,1,0:T(8,128)S(1)} %get-tuple-element.18) | data formatting | bytes 884736
  42.9 0.6 %copy.34 = f32[27,4,64]{2,1,0:T(4,128)} copy(f32[27,4,64]{2,1,0:T(4,128)S(1)} %get-tuple-element.19) | data formatting | bytes 55296
  (10 shorter events, 0.1 us)
Async XLA Ops:
  0.6 2.7 %copy-start.5 = (bf16[27,64,64]{2,1,0:T(8,128)(2,1)S(1)}, bf16[27,64,64]{2,1,0:T(8,128)(2,1)}, u32[]{:S(2)}) copy-start(bf16[27,64,64]{2,1,0:T(8,128)(2,1)} %param.10) | copy-start | bytes 663556
  2.4 0.7 %copy-start.6 = (bf16[27,4,64]{2,1,0:T(4,128)(2,1)S(1)}, bf16[27,4,64]{2,1,0:T(4,128)(2,1)}, u32[]{:S(2)}) copy-start(bf16[27,4,64]{2,1,0:T(4,128)(2,1)} %param.11) | copy-start | bytes 41476
  5.1 0.7 %copy-start = (f32[3,2,8,128]{3,2,1,0:T(8,128)S(1)}, f32[3,2,8,128]{3,2,1,0:T(8,128)}, u32[]{:S(2)}) copy-start(f32[3,2,8,128]{3,2,1,0:T(8,128)} %refs_6_.1) | copy-start | bytes 73732
  5.1 0.7 %copy-start.1 = (f32[3,2,8,128]{3,2,1,0:T(8,128)S(1)}, f32[3,2,8,128]{3,2,1,0:T(8,128)}, u32[]{:S(2)}) copy-start(f32[3,2,8,128]{3,2,1,0:T(8,128)} %refs_7_.1) | copy-start | bytes 73732
  5.1 0.8 %copy-start.2 = (f32[3,2,8,128]{3,2,1,0:T(8,128)S(1)}, f32[3,2,8,128]{3,2,1,0:T(8,128)}, u32[]{:S(2)}) copy-start(f32[3,2,8,128]{3,2,1,0:T(8,128)} %refs_8_.1) | copy-start | bytes 73732
  5.1 0.8 %copy-start.3 = (f32[3,2,8,128]{3,2,1,0:T(8,128)S(1)}, f32[3,2,8,128]{3,2,1,0:T(8,128)}, u32[]{:S(2)}) copy-start(f32[3,2,8,128]{3,2,1,0:T(8,128)} %refs_9_.1) | copy-start | bytes 73732
  5.1 0.7 %copy-start.4 = (bf16[3,2,8,128]{3,2,1,0:T(8,128)(2,1)S(1)}, bf16[3,2,8,128]{3,2,1,0:T(8,128)(2,1)}, u32[]{:S(2)}) copy-start(bf16[3,2,8,128]{3,2,1,0:T(8,128)(2,1)} %refs_0_.1) | copy-start | bytes 36868

commit v2 on v1

--- a/solution.py
+++ b/solution.py
@@ -79,13 +79,14 @@
 
 
 def kernel(n, cells, chunk, fchunk, *refs):
-    (feat, wf, wb, w1, w3, w3t, diff, pres, adv, forc,
-     pred_out, gfirst_out, gmid_out, glast_out,
+    (feat, w1_in, wm_in, wl_in, diff, pres, adv, forc,
+     pred_out, gf_out, gat_out,
+     wf, wb, w1, w3, w3t, stage, w3s,
      fc, fr, fl, mc, mr, ml, fsend, msend, fbase, fstage, fs, f1x, mid, m1x, pc, ph, psend,
      ogs, obase, og, mbx, fbs,
      red, redin, half, hin, gat, gfp, gfin, gfr,
      a_send, a_recv, p_send, p_recv, r_send, r_recv, s_send, s_recv, g_send, g_recv,
-     x_send, x_recv, q_send, q_recv, h_send, h_recv) = refs
+     x_send, x_recv, q_send, q_recv, h_send, h_recv, m_send, m_recv) = refs
     c = lax.axis_index("circ")
     ax = lax.axis_index("axial")
     grp = lax.axis_index("group")
@@ -115,26 +116,53 @@
     fc[ax] = x
     fsend[0] = pack_low(x[:, 0], x[:, 1])
     fsend[1] = pack_high(x[:, 0], x[:, 1])
+    lows, highs = [], []
     for g, ref in enumerate((diff, pres, adv, forc)):
         x = ref[...]
         mc[ax, 3 * g : 3 * g + 3] = x
-        msend[0, 3 * g : 3 * g + 3] = pack_low(x[:, 0], x[:, 1])
-        msend[1, 3 * g : 3 * g + 3] = pack_high(x[:, 0], x[:, 1])
+        for i in range(3):
+            lows.append(pack_low(x[i, 0], x[i, 1]))
+            highs.append(pack_high(x[i, 0], x[i, 1]))
+    for i in range(6):
+        msend[0, i] = jnp.concatenate(lows[2 * i : 2 * i + 2], axis=0).astype(BF16)
+        msend[1, i] = jnp.concatenate(highs[2 * i : 2 * i + 2], axis=0).astype(BF16)
+
+    stage[...] = jnp.zeros_like(stage)
+    for ch in range(3):
+        v = w1_in[ch].astype(F32)
+        for dd in range(9):
+            stage[dd * 16 + ch * 3 : dd * 16 + ch * 3 + 3, 0:64] = v[3 * dd : 3 * dd + 3]
+    w1[...] = stage[...].T[0:64].astype(BF16)
 
     pl.semaphore_wait(barrier, ndev - 1)
 
     fcopies = []
     mcopies = []
-    for out, cc, src_f, src_m, base in (
-        (fcopies, fc, None, None, 0), (mcopies, mc, None, None, 5)):
-        out.append(rcopy(cc.at[ax], cc.at[ax], a_send.at[base], a_recv.at[base], c, sib))
-    for out, lo, hi, snd, base in ((fcopies, fr, fl, fsend, 0), (mcopies, mr, ml, msend, 5)):
-        out.append(rcopy(snd.at[0], lo.at[ax], a_send.at[base + 1], a_recv.at[base + 1], left, ax))
-        out.append(rcopy(snd.at[1], hi.at[ax], a_send.at[base + 2], a_recv.at[base + 2], right, ax))
-        out.append(rcopy(snd.at[0], lo.at[ax], a_send.at[base + 3], a_recv.at[base + 3], left, sib))
-        out.append(rcopy(snd.at[1], hi.at[ax], a_send.at[base + 4], a_recv.at[base + 4], right, sib))
+    fcopies.append(rcopy(fc.at[ax], fc.at[ax], a_send.at[0], a_recv.at[0], c, sib))
+    fcopies.append(rcopy(fsend.at[0], fr.at[ax], a_send.at[1], a_recv.at[1], left, ax))
+    fcopies.append(rcopy(fsend.at[1], fl.at[ax], a_send.at[2], a_recv.at[2], right, ax))
+    fcopies.append(rcopy(fsend.at[0], fr.at[ax], a_send.at[3], a_recv.at[3], left, sib))
+    fcopies.append(rcopy(fsend.at[1], fl.at[ax], a_send.at[4], a_recv.at[4], right, sib))
+    mcopies.append(rcopy(mc.at[ax], mc.at[ax], a_send.at[5], a_recv.at[5], c, sib))
+    mcopies.append(rcopy(msend.at[0], mr.at[ax], a_send.at[6], a_recv.at[6], left, ax))
+    mcopies.append(rcopy(msend.at[1], ml.at[ax], a_send.at[7], a_recv.at[7], right, ax))
+    relays = [
+        rcopy(mr.at[ax], mr.at[ax], m_send.at[0], m_recv.at[0], c, sib),
+        rcopy(ml.at[ax], ml.at[ax], m_send.at[1], m_recv.at[1], c, sib),
+    ]
     for cp in fcopies + mcopies:
         cp.start()
+
+    for da in range(3):
+        for dr in range(3):
+            wf[da, dr * 64 : dr * 64 + 64] = jnp.concatenate(
+                [wm_in[9 * da + 3 * db + dr] for db in range(3)], axis=1)
+    w3s[...] = jnp.zeros_like(w3s)
+    for da in range(3):
+        for dr in range(3):
+            w3s[da, dr * 8 : dr * 8 + 4] = jnp.concatenate(
+                [wl_in[9 * da + 3 * db + dr].astype(F32) for db in range(3)], axis=1)
+    w3[...] = w3s[...].astype(BF16)
 
     for ref in (fs, f1x, m1x, og, mbx):
         ref[0] = jnp.zeros_like(ref[0])
@@ -163,9 +191,11 @@
                     v = fc[slab, ch, l, b : b + 1, :]
                 fbase[a, ch : ch + 1, j * 128 : (j + 1) * 128] = v
         base = fbase[a]
-        fstage[0:3, :] = from_behind(base)[0:3]
-        fstage[3:6, :] = base[0:3]
-        fstage[6:9, :] = from_ahead(base)[0:3]
+        low, high = from_behind(base), from_ahead(base)
+        for ch in range(3):
+            fstage[3 * ch : 3 * ch + 1, :] = low[ch : ch + 1]
+            fstage[3 * ch + 1 : 3 * ch + 2, :] = base[ch : ch + 1]
+            fstage[3 * ch + 2 : 3 * ch + 3, :] = high[ch : ch + 1]
         fs[a + 1] = fstage[...].astype(BF16)
 
     for a in range(4):
@@ -174,6 +204,11 @@
         first = jnp.tanh(dot(w1[...], xs)).astype(BF16)
         for db in range(3):
             f1x[a + 1, db * 64 : db * 64 + 64, :] = first[:, db * 128 : db * 128 + 1280]
+
+    for cp in mcopies:
+        cp.wait()
+    for cp in relays:
+        cp.start()
 
     for a in range(4):
         for t in range(5):
@@ -207,7 +242,16 @@
     for cp in pcopies:
         cp.start()
     pred_out[...] = pc[:, pl.ds(2 * ax, 2)].astype(BF16)
-    for cp in mcopies:
+    for dd in range(9):
+        for dr in range(3):
+            stage[dd * 16 + dr * 4 : dd * 16 + dr * 4 + 4, 0:64] = wl_in[dd * 3 + dr].astype(F32)
+        stage[dd * 16 + 12 : dd * 16 + 16, 0:64] = jnp.zeros((4, 64), F32)
+    w3t[...] = stage[...].T[0:64].astype(BF16)
+    for da in range(3):
+        for dr in range(3):
+            tall = jnp.concatenate([wm_in[9 * da + 3 * db + dr] for db in range(3)], axis=0)
+            wb[da, dr * 64 : dr * 64 + 64] = tall.T
+    for cp in relays:
         cp.wait()
     for cp in pcopies:
         cp.wait()
@@ -215,7 +259,7 @@
     def metric(index):
         layers = []
         for slab in range(2):
-            h = halo_tiles(mr[slab, index], ml[slab, index])
+            h = halo_tiles(*(ref[slab, index // 2].astype(F32)[index % 2 * 8 : index % 2 * 8 + 8] for ref in (mr, ml)))
             for l in range(2):
                 layers.append(jnp.concatenate([mc[slab, index, l], h[l]], axis=0))
         return jnp.stack(layers)
@@ -334,10 +378,10 @@
         xs = jnp.concatenate(
             [fs[own + l + da - 1, :, (2 + db) * 128 : (2 + db) * 128 + 1024]
              for da in range(3) for db in range(3)], axis=0)
-        term = dot_nt(fbs[l], xs)
+        term = dot_nt(xs, fbs[l])
         gf = term if gf is None else gf + term
-    gfp[0:64, :] = gf[:, 0:128]
-    gfp[64:128, 0:16] = gf[:, 128:144]
+    gfp[0:128, 0:64] = gf[0:128]
+    gfp[0:16, 64:128] = gf[128:144]
 
     def fscatter(j):
         peer = lax.rem(me + j, ndev)
@@ -411,14 +455,38 @@
 
     lax.fori_loop(0, n, end_forward, 0)
 
+    gat_out[...] = gat[...]
+
+    def end_fgather(j, carry):
+        fgather(j).wait()
+        return carry
+
+    lax.fori_loop(1, ndev, end_fgather, 0)
+    gf_out[...] = gfr[...]
+
+
+def unpack(pred_in, gf_in, gat_in, pred_out, gfirst_out, gmid_out, glast_out, gfirst_v, gmid_v, glast_v, sems):
+    hrows = gat_in.shape[1]
+    copies = [
+        pltpu.make_async_copy(src, dst, sems.at[i])
+        for i, (src, dst) in enumerate(
+            ((pred_in, pred_out), (gfirst_v, gfirst_out), (gmid_v, gmid_out), (glast_v, glast_out)))
+    ]
+    copies[0].start()
+    for dd in range(9):
+        for ch in range(3):
+            row = dd % 8 * 16 + ch * 3
+            gfirst_v[ch, 3 * dd : 3 * dd + 3, :] = gf_in[row : row + 3, dd // 8 * 64 : dd // 8 * 64 + 64]
+    copies[1].start()
+
     def rows_of(start, count, lanes):
         hr = hrows
         if start + count <= hr:
-            return gat[0, start : start + count, lanes : lanes + 64]
+            return gat_in[0, start : start + count, lanes : lanes + 64]
         if start >= hr:
-            return gat[1, start - hr : start - hr + count, lanes : lanes + 64]
+            return gat_in[1, start - hr : start - hr + count, lanes : lanes + 64]
         return jnp.concatenate(
-            [gat[0, start:hr, lanes : lanes + 64], gat[1, 0 : start + count - hr, lanes : lanes + 64]], axis=0)
+            [gat_in[0, start:hr, lanes : lanes + 64], gat_in[1, 0 : start + count - hr, lanes : lanes + 64]], axis=0)
 
     for dd in range(9):
         if dd < 8:
@@ -427,29 +495,20 @@
             lblock = rows_of(928, 16, 0).astype(F32)
         for dr in range(3):
             k = dd * 3 + dr
-            glast_out[k] = lblock[dr * 4 : dr * 4 + 4]
+            glast_v[k] = lblock[dr * 4 : dr * 4 + 4]
             if dd < 8:
-                gmid_out[k] = rows_of(dd // 2 * 192 + dr * 64, 64, dd % 2 * 64).astype(F32)
+                gmid_v[k] = rows_of(dd // 2 * 192 + dr * 64, 64, dd % 2 * 64).astype(F32)
             elif dr == 0:
-                gmid_out[k] = rows_of(768, 64, 0).astype(F32)
+                gmid_v[k] = rows_of(768, 64, 0).astype(F32)
             elif dr == 1:
-                gmid_out[k, 0:32] = rows_of(832, 32, 0).astype(F32)
-                gmid_out[k, 32:64] = rows_of(768, 32, 64).astype(F32)
+                gmid_v[k, 0:32] = rows_of(832, 32, 0).astype(F32)
+                gmid_v[k, 32:64] = rows_of(768, 32, 64).astype(F32)
             else:
-                gmid_out[k] = rows_of(800, 64, 64).astype(F32)
-
-    def end_fgather(j, carry):
-        fgather(j).wait()
-        return carry
-
-    lax.fori_loop(1, ndev, end_fgather, 0)
-    g0 = gfr[0:64, :]
-    g1 = gfr[64:128, :]
-    for dd in range(9):
-        src = g0 if dd < 8 else g1
-        for dr in range(3):
-            start = (dd * 16) % 128 + dr * 3
-            gfirst_out[dd * 3 + dr] = src[:, start : start + 3]
+                gmid_v[k] = rows_of(800, 64, 64).astype(F32)
+    copies[2].start()
+    copies[3].start()
+    for cp in copies:
+        cp.wait()
 
 
 def body(features, w_first, w_middle, w_last, diffusion, pressure, advection, forcing):
@@ -462,23 +521,14 @@
     fchunk = max(8, 128 // ndev)
     frows = fchunk * ndev
 
-    w = w_middle.reshape(3, 3, 3, 64, 64)
-    wf = w.transpose(0, 2, 3, 1, 4).reshape(3, 192, 192)
-    wb = w.transpose(0, 2, 4, 1, 3).reshape(3, 192, 192)
-    w1 = w_first.reshape(3, 3, 3, 64, 3).transpose(3, 0, 1, 2, 4).reshape(64, 9, 9)
-    w1 = jnp.pad(w1, ((0, 0), (0, 0), (0, 7))).reshape(64, 144)
-    wl = w_last.reshape(3, 3, 3, 4, 64)
-    w3 = jnp.pad(wl.transpose(0, 2, 3, 1, 4), ((0, 0), (0, 0), (0, 4), (0, 0), (0, 0))).reshape(3, 24, 192)
-    w3 = jnp.pad(w3, ((0, 0), (0, 8), (0, 0)))
-    w3t = wl.transpose(4, 0, 1, 2, 3).reshape(64, 9, 12)
-    w3t = jnp.pad(w3t, ((0, 0), (0, 0), (0, 4))).reshape(64, 144)
-
     V = pltpu.VMEM
     dma = pltpu.SemaphoreType.DMA
     scratch = [
+        V((3, 192, 192), BF16), V((3, 192, 192), BF16), V((64, 144), BF16), V((3, 32, 192), BF16),
+        V((64, 144), BF16), V((144, 128), F32), V((3, 32, 192), F32),
         V((2, 3, 2, 8, 128), F32), V((2, 3, 8, 128), F32), V((2, 3, 8, 128), F32),
-        V((2, 12, 2, 8, 128), F32), V((2, 12, 8, 128), F32), V((2, 12, 8, 128), F32),
-        V((2, 3, 8, 128), F32), V((2, 12, 8, 128), F32),
+        V((2, 12, 2, 8, 128), F32), V((2, 6, 16, 128), BF16), V((2, 6, 16, 128), BF16),
+        V((2, 3, 8, 128), F32), V((2, 6, 16, 128), BF16),
         V((4, 8, 1792), F32), V((16, 1792), F32), V((6, 16, 1792), BF16),
         V((6, 192, 1280), BF16), V((4, 64, 1280), BF16), V((6, 192, 1024), BF16),
         V((4, 4, 8, 128), F32), V((2, 4, 2, 8, 128), F32), V((2, 4, 2, 8, 128), F32),
@@ -487,24 +537,37 @@
         V((rrows, 128), BF16), V((rrows // 2, 128), BF16), V((rrows // 2, 128), BF16),
         V((n, chunk, 128), BF16), V((2, rrows // 2, 128), BF16),
         V((frows, 128), F32), V((ndev, fchunk, 128), F32), V((frows, 128), F32),
-        dma((10,)), dma((10,)), dma((2,)), dma((2,)), dma, dma, dma((n,)), dma((n,)), dma((n,)), dma((n,)),
-        dma((ndev,)), dma((ndev,)), dma((ndev,)), dma((ndev,)), dma((n,)), dma((n,)),
+        dma((8,)), dma((8,)), dma((2,)), dma((2,)), dma, dma, dma((n,)), dma((n,)), dma((n,)), dma((n,)),
+        dma((ndev,)), dma((ndev,)), dma((ndev,)), dma((ndev,)), dma((n,)), dma((n,)), dma((2,)), dma((2,)),
     ]
     vm = pl.BlockSpec(memory_space=pltpu.VMEM)
-    return pl.pallas_call(
+    pred, gf, gat = pl.pallas_call(
         functools.partial(kernel, n, cells, chunk, fchunk),
         out_shape=(
             jax.ShapeDtypeStruct((4, rows, cols, depth), BF16),
-            jax.ShapeDtypeStruct((27, 64, 3), F32),
+            jax.ShapeDtypeStruct((frows, 128), F32),
+            jax.ShapeDtypeStruct((2, rrows // 2, 128), BF16),
+        ),
+        in_specs=[vm] * 8,
+        out_specs=(vm,) * 3,
+        scratch_shapes=scratch,
+        compiler_params=pltpu.CompilerParams(
+            collective_id=0, has_side_effects=True, vmem_limit_bytes=48 * 1024 * 1024),
+    )(features, w_first.transpose(2, 0, 1), w_middle, w_last, diffusion, pressure, advection, forcing)
+    hbm = pl.BlockSpec(memory_space=pl.ANY)
+    predicted, gfirst, gmid, glast = pl.pallas_call(
+        unpack,
+        out_shape=(
+            jax.ShapeDtypeStruct((4, rows, cols, depth), BF16),
+            jax.ShapeDtypeStruct((3, 27, 64), F32),
             jax.ShapeDtypeStruct((27, 64, 64), F32),
             jax.ShapeDtypeStruct((27, 4, 64), F32),
         ),
-        in_specs=[vm] * 10,
-        out_specs=(vm,) * 4,
-        scratch_shapes=scratch,
-        compiler_params=pltpu.CompilerParams(
-            collective_id=0, has_side_effects=True, vmem_limit_bytes=48 * 1024 * 1024),
-    )(features, wf, wb, w1, w3, w3t, diffusion, pressure, advection, forcing)
+        in_specs=[vm] * 3,
+        out_specs=(hbm,) * 4,
+        scratch_shapes=[V((3, 27, 64), F32), V((27, 64, 64), F32), V((27, 4, 64), F32), dma((4,))],
+    )(pred, gf, gat)
+    return predicted, gfirst.transpose(1, 2, 0), gmid, glast
 
 
 def solution(mesh):

time: 43.8 us -> 44.9 us (1.025)
  Pallas kernels: 34.5 us -> 35.6 us
    unnamed x18 -> x22, local copies, waits for them, and re-layouts: 3.2 us -> 8.06 us
    reshape x10 -> x0, local copies, waits for them, and re-layouts: 3.95 us -> none  [the longest x2 1.35 us: body(): w = w_middle.reshape(3, 3, 3, 64, 64)]
    pallas_call x0 -> x1, Pallas kernels: none -> 2.09 us  [body(): pl.pallas_call(unpack, out_shape=(jax.ShapeDtypeStruct((4, rows, cols, de...]
    pallas_call x1, Pallas kernels: 34.5 us -> 33.5 us  [body(): pl.pallas_call(functools.partial(kernel, n, cells, chunk, fchunk), out_sh...]
    pallas_call x1 -> x0, local copies, waits for them, and re-layouts: 0.99 us -> none  [body(): pl.pallas_call(functools.partial(kernel, n, cells, chunk, fchunk), out_sh...]
where the time goes in v2:
time: 44.9 us; the launch traced here: 44.3 us
  Pallas kernels  35.6 us (79%)
  local copies, waits for them, and re-layouts  8.06 us (18%)
  between operations  0.67 us (1%)
    pallas_call x1, Pallas kernels, body(): pl.pallas_call(functools.partial(kernel, n, cells, chunk, fchunk), out_sh...  33.5 us
    unnamed x22, local copies, waits for them, and re-layouts  8.06 us
    pallas_call x1, Pallas kernels, body(): pl.pallas_call(unpack, out_shape=(jax.ShapeDtypeStruct((4, rows, cols, de...  2.09 us

profile of v2, /device:TPU:0, one launch (start us, length us, event | category | flops | bytes accessed | tf_op | source)
XLA Modules:
  0.0 44.3 jit_solution(12756970906923645698)
XLA Ops:
  0.6 0.0 copy-start
  0.6 1.0 %copy-done = bf16[27,64,64]{2,1,0:T(8,128)(2,1)S(1)} copy-done((bf16[27,64,64]{2,1,0:T(8,128)(2,1)S(1)}, bf16[27,64,64]{2,1,0:T(8,128)(2,1)}, u32[]{:S(2)}) %copy-start) | copy-done | bytes 221208
  1.6 0.0 copy-start.3
  1.6 0.7 %copy-done.3 = bf16[27,4,64]{2,1,0:T(4,128)(2,1)S(1)} copy-done((bf16[27,4,64]{2,1,0:T(4,128)(2,1)S(1)}, bf16[27,4,64]{2,1,0:T(4,128)(2,1)}, u32[]{:S(2)}) %copy-start.3) | copy-done | bytes 13848
  2.4 0.0 copy-start.4
  2.4 0.7 %copy-done.4 = bf16[27,64,3]{1,0,2:T(8,128)(2,1)S(1)} copy-done((bf16[27,64,3]{1,0,2:T(8,128)(2,1)S(1)}, bf16[27,64,3]{1,0,2:T(8,128)(2,1)}, u32[]{:S(2)}) %copy-start.4) | copy-done | bytes 10392
  3.1 0.0 copy-start.5
  3.1 0.7 %copy-done.5 = f32[3,2,8,128]{3,2,1,0:T(8,128)S(1)} copy-done((f32[3,2,8,128]{3,2,1,0:T(8,128)S(1)}, f32[3,2,8,128]{3,2,1,0:T(8,128)}, u32[]{:S(2)}) %copy-start.5) | copy-done | bytes 24600
  3.9 0.0 copy-start.6
  3.9 0.7 %copy-done.6 = f32[3,2,8,128]{3,2,1,0:T(8,128)S(1)} copy-done((f32[3,2,8,128]{3,2,1,0:T(8,128)S(1)}, f32[3,2,8,128]{3,2,1,0:T(8,128)}, u32[]{:S(2)}) %copy-start.6) | copy-done | bytes 24600
  4.6 0.0 copy-start.7
  4.6 0.7 %copy-done.7 = f32[3,2,8,128]{3,2,1,0:T(8,128)S(1)} copy-done((f32[3,2,8,128]{3,2,1,0:T(8,128)S(1)}, f32[3,2,8,128]{3,2,1,0:T(8,128)}, u32[]{:S(2)}) %copy-start.7) | copy-done | bytes 24600
  5.3 0.0 copy-start.8
  5.3 0.7 %copy-done.8 = f32[3,2,8,128]{3,2,1,0:T(8,128)S(1)} copy-done((f32[3,2,8,128]{3,2,1,0:T(8,128)S(1)}, f32[3,2,8,128]{3,2,1,0:T(8,128)}, u32[]{:S(2)}) %copy-start.8) | copy-done | bytes 24600
  6.1 0.0 copy-start.10
  6.1 0.7 %copy-done.10 = bf16[3,2,8,128]{3,2,1,0:T(8,128)(2,1)S(1)} copy-done((bf16[3,2,8,128]{3,2,1,0:T(8,128)(2,1)S(1)}, bf16[3,2,8,128]{3,2,1,0:T(8,128)(2,1)}, u32[]{:S(2)}) %copy-start.10) | copy-done | bytes 12312
  6.8 33.5 %shard_map.111 = (bf16[4,2,8,128]{3,2,1,0:T(8,128)(2,1)S(1)}, f32[128,128]{1,0:T(8,128)S(1)}, bf16[2,512,128]{2,1,0:T(8,128)(2,1)S(1)}) custom-call(bf16[3,2,8,128]{3,2,1,0:T(8,128)(2,1)S(1)} %copy-done.10, bf16[3,27,64]{2,1,0:T(8,128)(2,1)S(1)} %bitcast.2, bf16[27,64,64]{2,1,0:T(8,128)(2,1)S(1)} %copy-done, bf16[27,4,64]{2,1,0:T(4,128)(2,1)S(1)} %copy-done.3, ...), custom_call_target="tpu_custom_call" | custom-call | tf_op jit(solution)/shard_map/pallas_call | solution.py:544
  40.3 0.0 copy-start.1
  40.3 0.7 %copy-done.1 = bf16[2,512,128]{2,1,0:T(8,128)(2,1)} copy-done((bf16[2,512,128]{2,1,0:T(8,128)(2,1)}, bf16[2,512,128]{2,1,0:T(8,128)(2,1)S(1)}, u32[]{:S(2)}) %copy-start.1) | copy-done | bytes 262168
  41.0 0.0 copy-start.2
  41.0 0.6 %copy-done.2 = f32[128,128]{1,0:T(8,128)} copy-done((f32[128,128]{1,0:T(8,128)}, f32[128,128]{1,0:T(8,128)S(1)}, u32[]{:S(2)}) %copy-start.2) | copy-done | bytes 65560
  41.6 0.0 copy-start.9
  41.6 0.6 %copy-done.9 = bf16[4,2,8,128]{3,2,1,0:T(8,128)(2,1)} copy-done((bf16[4,2,8,128]{3,2,1,0:T(8,128)(2,1)}, bf16[4,2,8,128]{3,2,1,0:T(8,128)(2,1)S(1)}, u32[]{:S(2)}) %copy-start.9) | copy-done | bytes 16408
  42.2 2.1 %shard_map.112 = (bf16[4,2,8,128]{3,2,1,0:T(8,128)(2,1)}, f32[3,27,64]{2,1,0:T(8,128)}, f32[27,64,64]{2,1,0:T(8,128)}, f32[27,4,64]{2,1,0:T(4,128)}) custom-call(bf16[4,2,8,128]{3,2,1,0:T(8,128)(2,1)} %copy-done.9, f32[128,128]{1,0:T(8,128)} %copy-done.2, bf16[2,512,128]{2,1,0:T(8,128)(2,1)} %copy-done.1), custom_call_target="tpu_custom_call" | custom-call | tf_op jit(solution)/shard_map/pallas_call | solution.py:558
Async XLA Ops:
  0.6 1.0 %copy-start = (bf16[27,64,64]{2,1,0:T(8,128)(2,1)S(1)}, bf16[27,64,64]{2,1,0:T(8,128)(2,1)}, u32[]{:S(2)}) copy-start(bf16[27,64,64]{2,1,0:T(8,128)(2,1)} %refs_2_.1) | copy-start | bytes 663556
  1.6 0.7 %copy-start.3 = (bf16[27,4,64]{2,1,0:T(4,128)(2,1)S(1)}, bf16[27,4,64]{2,1,0:T(4,128)(2,1)}, u32[]{:S(2)}) copy-start(bf16[27,4,64]{2,1,0:T(4,128)(2,1)} %refs_3_.1) | copy-start | bytes 41476
  2.4 0.7 %copy-start.4 = (bf16[27,64,3]{1,0,2:T(8,128)(2,1)S(1)}, bf16[27,64,3]{1,0,2:T(8,128)(2,1)}, u32[]{:S(2)}) copy-start(bf16[27,64,3]{1,0,2:T(8,128)(2,1)} %param.9) | copy-start | bytes 31108
  3.1 0.7 %copy-start.5 = (f32[3,2,8,128]{3,2,1,0:T(8,128)S(1)}, f32[3,2,8,128]{3,2,1,0:T(8,128)}, u32[]{:S(2)}) copy-start(f32[3,2,8,128]{3,2,1,0:T(8,128)} %refs_4_.1) | copy-start | bytes 73732
  3.9 0.7 %copy-start.6 = (f32[3,2,8,128]{3,2,1,0:T(8,128)S(1)}, f32[3,2,8,128]{3,2,1,0:T(8,128)}, u32[]{:S(2)}) copy-start(f32[3,2,8,128]{3,2,1,0:T(8,128)} %refs_5_.1) | copy-start | bytes 73732
  4.6 0.7 %copy-start.7 = (f32[3,2,8,128]{3,2,1,0:T(8,128)S(1)}, f32[3,2,8,128]{3,2,1,0:T(8,128)}, u32[]{:S(2)}) copy-start(f32[3,2,8,128]{3,2,1,0:T(8,128)} %refs_6_.1) | copy-start | bytes 73732
  5.3 0.7 %copy-start.8 = (f32[3,2,8,128]{3,2,1,0:T(8,128)S(1)}, f32[3,2,8,128]{3,2,1,0:T(8,128)}, u32[]{:S(2)}) copy-start(f32[3,2,8,128]{3,2,1,0:T(8,128)} %refs_7_.1) | copy-start | bytes 73732
  6.1 0.7 %copy-start.10 = (bf16[3,2,8,128]{3,2,1,0:T(8,128)(2,1)S(1)}, bf16[3,2,8,128]{3,2,1,0:T(8,128)(2,1)}, u32[]{:S(2)}) copy-start(bf16[3,2,8,128]{3,2,1,0:T(8,128)(2,1)} %refs_0_.1) | copy-start | bytes 36868
  40.3 0.7 %copy-start.1 = (bf16[2,512,128]{2,1,0:T(8,128)(2,1)}, bf16[2,512,128]{2,1,0:T(8,128)(2,1)S(1)}, u32[]{:S(2)}) copy-start(bf16[2,512,128]{2,1,0:T(8,128)(2,1)S(1)} %get-tuple-element.13.gat_in) | copy-start | bytes 786436
  41.0 0.6 %copy-start.2 = (f32[128,128]{1,0:T(8,128)}, f32[128,128]{1,0:T(8,128)S(1)}, u32[]{:S(2)}) copy-start(f32[128,128]{1,0:T(8,128)S(1)} %get-tuple-element.12.gf_in) | copy-start | bytes 196612
  41.6 0.6 %copy-start.9 = (bf16[4,2,8,128]{3,2,1,0:T(8,128)(2,1)}, bf16[4,2,8,128]{3,2,1,0:T(8,128)(2,1)S(1)}, u32[]{:S(2)}) copy-start(bf16[4,2,8,128]{3,2,1,0:T(8,128)(2,1)S(1)} %get-tuple-element.11.pred_in) | copy-start | bytes 49156

commit v3 on v2

--- a/solution.py
+++ b/solution.py
@@ -10,7 +10,7 @@
 MESH = pl.DeviceIdType.MESH
 F32 = jnp.float32
 BF16 = jnp.bfloat16
-HALO = 4
+VMEM_LIMIT = 62 * 1024 * 1024
 
 
 def dot(a, b):
@@ -78,46 +78,52 @@
     return low_half(right, left), roll4(low_half(left, right))
 
 
-def kernel(n, cells, chunk, fchunk, *refs):
-    (feat, w1_in, wm_in, wl_in, diff, pres, adv, forc,
-     pred_out, gf_out, gat_out,
+def kernel(n, cells, chunk, *refs):
+    (*sources,
+     pred_out, gat_out,
+     feat, w1_in, wm_in, wl_in, diff, pres, adv, forc, i_sem,
      wf, wb, w1, w3, w3t, stage, w3s,
      fc, fr, fl, mc, mr, ml, fsend, msend, fbase, fstage, fs, f1x, mid, m1x, pc, ph, psend,
      ogs, obase, og, mbx, fbs,
-     red, redin, half, hin, gat, gfp, gfin, gfr,
+     red, redin, half, hin, gat,
      a_send, a_recv, p_send, p_recv, r_send, r_recv, s_send, s_recv, g_send, g_recv,
-     x_send, x_recv, q_send, q_recv, h_send, h_recv, m_send, m_recv) = refs
+     h_send, h_recv, m_send, m_recv) = refs
     c = lax.axis_index("circ")
     ax = lax.axis_index("axial")
     grp = lax.axis_index("group")
     sib = 1 - ax
     right = lax.rem(c + 1, n)
     left = lax.rem(c + n - 1, n)
-    ndev = 2 * n
-    me = c * 2 + ax
-
-    def device(i):
-        return (grp, i // 2, lax.rem(i, 2))
-
     def rcopy(src, dst, ss, rs, circ, axial):
         return pltpu.make_async_remote_copy(
             src_ref=src, dst_ref=dst, send_sem=ss, recv_sem=rs,
             device_id=(grp, circ, axial), device_id_type=MESH)
 
+    loads = [
+        pltpu.make_async_copy(src, dst, i_sem.at[i])
+        for i, (src, dst) in enumerate(zip(sources, (feat, w1_in, wm_in, wl_in, diff, pres, adv, forc)))
+    ]
+    for i in (0, 1, 4, 5, 6, 7, 2, 3):
+        loads[i].start()
+
     barrier = pltpu.get_barrier_semaphore()
 
     def greet(j, carry):
-        pl.semaphore_signal(barrier, inc=1, device_id=device(lax.rem(me + j, ndev)), device_id_type=MESH)
+        pl.semaphore_signal(barrier, inc=1, device_id=(grp, lax.rem(c + j, n), ax), device_id_type=MESH)
         return carry
 
-    lax.fori_loop(1, ndev, greet, 0)
-
+    for cc in (left, right, c):
+        pl.semaphore_signal(barrier, inc=1, device_id=(grp, cc, sib), device_id_type=MESH)
+    lax.fori_loop(1, n, greet, 0)
+
+    loads[0].wait()
     x = feat[...].astype(F32)
     fc[ax] = x
     fsend[0] = pack_low(x[:, 0], x[:, 1])
     fsend[1] = pack_high(x[:, 0], x[:, 1])
     lows, highs = [], []
     for g, ref in enumerate((diff, pres, adv, forc)):
+        loads[4 + g].wait()
         x = ref[...]
         mc[ax, 3 * g : 3 * g + 3] = x
         for i in range(3):
@@ -128,13 +134,14 @@
         msend[1, i] = jnp.concatenate(highs[2 * i : 2 * i + 2], axis=0).astype(BF16)
 
     stage[...] = jnp.zeros_like(stage)
+    loads[1].wait()
     for ch in range(3):
         v = w1_in[ch].astype(F32)
         for dd in range(9):
             stage[dd * 16 + ch * 3 : dd * 16 + ch * 3 + 3, 0:64] = v[3 * dd : 3 * dd + 3]
     w1[...] = stage[...].T[0:64].astype(BF16)
 
-    pl.semaphore_wait(barrier, ndev - 1)
+    pl.semaphore_wait(barrier, n + 2)
 
     fcopies = []
     mcopies = []
@@ -153,6 +160,8 @@
     for cp in fcopies + mcopies:
         cp.start()
 
+    loads[2].wait()
+    loads[3].wait()
     for da in range(3):
         for dr in range(3):
             wf[da, dr * 64 : dr * 64 + 64] = jnp.concatenate(
@@ -168,8 +177,8 @@
         ref[0] = jnp.zeros_like(ref[0])
         ref[5] = jnp.zeros_like(ref[5])
     fstage[...] = jnp.zeros_like(fstage)
-    red[944:1024] = jnp.zeros((80, 128), BF16)
-    gfp[...] = jnp.zeros_like(gfp)
+    if red.shape[0] > 1024:
+        red[1024:] = jnp.zeros_like(red[1024:])
     fbase[...] = jnp.zeros_like(fbase)
     obase[...] = jnp.zeros_like(obase)
 
@@ -346,8 +355,35 @@
     red[928:944] = jnp.concatenate([lastl, jnp.zeros_like(lastl)], axis=1).astype(BF16)
 
     hrows = red.shape[0] // 2
-    swap = rcopy(red.at[pl.ds(pl.multiple_of(sib * hrows, 16), hrows)], redin, r_send, r_recv, c, sib)
-    swap.start()
+    early = (944 - hrows) // chunk
+    erows = early * chunk
+
+    def swap(k):
+        start, count = ((0, erows), (erows, hrows - erows))[k]
+        return rcopy(red.at[pl.ds(pl.multiple_of(sib * hrows + start, 16), count)], redin.at[start : start + count],
+                     r_send.at[k], r_recv.at[k], c, sib)
+
+    def merge(k):
+        start, count = ((0, erows), (erows, hrows - erows))[k]
+        swap(k).wait()
+        mine = red[pl.ds(pl.multiple_of(ax * hrows + start, 16), count)].astype(F32)
+        half[start : start + count] = (mine + redin[start : start + count].astype(F32)).astype(BF16)
+
+    def scatter(j):
+        peer = lax.rem(c + j, n)
+        return rcopy(half.at[pl.ds(pl.multiple_of(peer * chunk, 16), chunk)], hin.at[j],
+                     s_send.at[j], s_recv.at[j], peer, ax)
+
+    def start_scatter(first):
+        def step(j, carry):
+            @pl.when((lax.rem(c + j, n) < early) == first)
+            def _():
+                scatter(j).start()
+            return carry
+
+        lax.fori_loop(1, n, step, 0)
+
+    swap(0).start()
 
     def first_back(l):
         acc = None
@@ -358,20 +394,8 @@
         return (shift_sum_back(acc, 64) * (1.0 - ff * ff)).astype(BF16)
 
     fbs[0] = first_back(0)
-    swap.wait()
-    half[...] = (red[pl.ds(pl.multiple_of(ax * hrows, 16), hrows)].astype(F32) + redin[...].astype(F32)).astype(BF16)
-
-    def scatter(j):
-        peer = lax.rem(c + j, n)
-        return rcopy(half.at[pl.ds(pl.multiple_of(peer * chunk, 16), chunk)], hin.at[j],
-                     s_send.at[j], s_recv.at[j], peer, ax)
-
-    def start_scatter(j, carry):
-        scatter(j).start()
-        return carry
-
-    lax.fori_loop(1, n, start_scatter, 0)
-
+    merge(0)
+    start_scatter(True)
     fbs[1] = first_back(1)
     gf = None
     for l in range(2):
@@ -380,20 +404,11 @@
              for da in range(3) for db in range(3)], axis=0)
         term = dot_nt(xs, fbs[l])
         gf = term if gf is None else gf + term
-    gfp[0:128, 0:64] = gf[0:128]
-    gfp[0:16, 64:128] = gf[128:144]
-
-    def fscatter(j):
-        peer = lax.rem(me + j, ndev)
-        return pltpu.make_async_remote_copy(
-            src_ref=gfp.at[pl.ds(pl.multiple_of(peer * fchunk, 8), fchunk)], dst_ref=gfin.at[j],
-            send_sem=x_send.at[j], recv_sem=x_recv.at[j], device_id=device(peer), device_id_type=MESH)
-
-    def start_fscatter(j, carry):
-        fscatter(j).start()
-        return carry
-
-    lax.fori_loop(1, ndev, start_fscatter, 0)
+    tail = jnp.concatenate([gf[80:144], jnp.zeros((16, 64), F32)], axis=0)
+    red[944:1024] = jnp.concatenate([gf[0:80], tail], axis=1).astype(BF16)
+    swap(1).start()
+    merge(1)
+    start_scatter(False)
 
     def add_chunk(j, total):
         scatter(j).wait()
@@ -421,27 +436,6 @@
 
     forward(0).start()
 
-    def fadd(j, total):
-        fscatter(j).wait()
-        return total + gfin[j]
-
-    fmine = gfp[pl.ds(pl.multiple_of(me * fchunk, 8), fchunk)]
-    fhere = pl.multiple_of(me * fchunk, 8)
-    gfr[pl.ds(fhere, fchunk)] = lax.fori_loop(1, ndev, fadd, fmine)
-
-    def fgather(j):
-        peer = lax.rem(me + j, ndev)
-        part = gfr.at[pl.ds(fhere, fchunk)]
-        return pltpu.make_async_remote_copy(
-            src_ref=part, dst_ref=part, send_sem=q_send.at[j], recv_sem=q_recv.at[j],
-            device_id=device(peer), device_id_type=MESH)
-
-    def start_fgather(j, carry):
-        fgather(j).start()
-        return carry
-
-    lax.fori_loop(1, ndev, start_fgather, 0)
-
     def relay(j, carry):
         gather(j).wait()
         forward(j).start()
@@ -457,15 +451,10 @@
 
     gat_out[...] = gat[...]
 
-    def end_fgather(j, carry):
-        fgather(j).wait()
-        return carry
-
-    lax.fori_loop(1, ndev, end_fgather, 0)
-    gf_out[...] = gfr[...]
-
-
-def unpack(pred_in, gf_in, gat_in, pred_out, gfirst_out, gmid_out, glast_out, gfirst_v, gmid_v, glast_v, sems):
+
+def unpack(pred_in, gat_hbm, pred_out, gfirst_out, gmid_out, glast_out, gat_in, gfirst_v, gmid_v, glast_v, sems):
+    load = pltpu.make_async_copy(gat_hbm, gat_in, sems.at[4])
+    load.start()
     hrows = gat_in.shape[1]
     copies = [
         pltpu.make_async_copy(src, dst, sems.at[i])
@@ -473,12 +462,7 @@
             ((pred_in, pred_out), (gfirst_v, gfirst_out), (gmid_v, gmid_out), (glast_v, glast_out)))
     ]
     copies[0].start()
-    for dd in range(9):
-        for ch in range(3):
-            row = dd % 8 * 16 + ch * 3
-            gfirst_v[ch, 3 * dd : 3 * dd + 3, :] = gf_in[row : row + 3, dd // 8 * 64 : dd // 8 * 64 + 64]
-    copies[1].start()
-
+    load.wait()
     def rows_of(start, count, lanes):
         hr = hrows
         if start + count <= hr:
@@ -506,6 +490,13 @@
             else:
                 gmid_v[k] = rows_of(800, 64, 64).astype(F32)
     copies[2].start()
+    g0 = rows_of(944, 80, 0).astype(F32)
+    g1 = rows_of(944, 64, 64).astype(F32)
+    for dd in range(9):
+        for ch in range(3):
+            row = dd % 5 * 16 + ch * 3
+            gfirst_v[ch, 3 * dd : 3 * dd + 3, :] = (g0 if dd < 5 else g1)[row : row + 3]
+    copies[1].start()
     copies[3].start()
     for cp in copies:
         cp.wait()
@@ -513,17 +504,16 @@
 
 def body(features, w_first, w_middle, w_last, diffusion, pressure, advection, forcing):
     n = lax.axis_size("circ")
-    ndev = 2 * n
     rows, cols, depth = features.shape[1:]
-    cells = rows * cols * depth * ndev
+    cells = rows * cols * depth * n * 2
     chunk = max(16, 512 // n)
     rrows = chunk * n * 2
-    fchunk = max(8, 128 // ndev)
-    frows = fchunk * ndev
 
     V = pltpu.VMEM
     dma = pltpu.SemaphoreType.DMA
-    scratch = [
+    held = (features, w_first.transpose(2, 0, 1), w_middle, w_last, diffusion, pressure, advection, forcing)
+    scratch = [V(x.shape, x.dtype) for x in held] + [
+        dma((8,)),
         V((3, 192, 192), BF16), V((3, 192, 192), BF16), V((64, 144), BF16), V((3, 32, 192), BF16),
         V((64, 144), BF16), V((144, 128), F32), V((3, 32, 192), F32),
         V((2, 3, 2, 8, 128), F32), V((2, 3, 8, 128), F32), V((2, 3, 8, 128), F32),
@@ -536,24 +526,22 @@
         V((6, 192, 1024), BF16), V((2, 64, 1024), BF16),
         V((rrows, 128), BF16), V((rrows // 2, 128), BF16), V((rrows // 2, 128), BF16),
         V((n, chunk, 128), BF16), V((2, rrows // 2, 128), BF16),
-        V((frows, 128), F32), V((ndev, fchunk, 128), F32), V((frows, 128), F32),
-        dma((8,)), dma((8,)), dma((2,)), dma((2,)), dma, dma, dma((n,)), dma((n,)), dma((n,)), dma((n,)),
-        dma((ndev,)), dma((ndev,)), dma((ndev,)), dma((ndev,)), dma((n,)), dma((n,)), dma((2,)), dma((2,)),
+        dma((8,)), dma((8,)), dma((2,)), dma((2,)), dma((2,)), dma((2,)), dma((n,)), dma((n,)), dma((n,)), dma((n,)),
+        dma((n,)), dma((n,)), dma((2,)), dma((2,)),
     ]
     vm = pl.BlockSpec(memory_space=pltpu.VMEM)
-    pred, gf, gat = pl.pallas_call(
-        functools.partial(kernel, n, cells, chunk, fchunk),
+    pred, gat = pl.pallas_call(
+        functools.partial(kernel, n, cells, chunk),
         out_shape=(
             jax.ShapeDtypeStruct((4, rows, cols, depth), BF16),
-            jax.ShapeDtypeStruct((frows, 128), F32),
             jax.ShapeDtypeStruct((2, rrows // 2, 128), BF16),
         ),
-        in_specs=[vm] * 8,
-        out_specs=(vm,) * 3,
+        in_specs=[pl.BlockSpec(memory_space=pltpu.HBM)] * 8,
+        out_specs=(vm,) * 2,
         scratch_shapes=scratch,
         compiler_params=pltpu.CompilerParams(
-            collective_id=0, has_side_effects=True, vmem_limit_bytes=48 * 1024 * 1024),
-    )(features, w_first.transpose(2, 0, 1), w_middle, w_last, diffusion, pressure, advection, forcing)
+            collective_id=0, has_side_effects=True, vmem_limit_bytes=VMEM_LIMIT),
+    )(*held)
     hbm = pl.BlockSpec(memory_space=pl.ANY)
     predicted, gfirst, gmid, glast = pl.pallas_call(
         unpack,
@@ -563,10 +551,12 @@
             jax.ShapeDtypeStruct((27, 64, 64), F32),
             jax.ShapeDtypeStruct((27, 4, 64), F32),
         ),
-        in_specs=[vm] * 3,
+        in_specs=[pl.BlockSpec(memory_space=pltpu.HBM)] * 2,
         out_specs=(hbm,) * 4,
-        scratch_shapes=[V((3, 27, 64), F32), V((27, 64, 64), F32), V((27, 4, 64), F32), dma((4,))],
-    )(pred, gf, gat)
+        scratch_shapes=[
+            V(gat.shape, BF16), V((3, 27, 64), F32), V((27, 64, 64), F32), V((27, 4, 64), F32), dma((5,))],
+        compiler_params=pltpu.CompilerParams(vmem_limit_bytes=VMEM_LIMIT),
+    )(pred, gat)
     return predicted, gfirst.transpose(1, 2, 0), gmid, glast
 
 

time: 44.9 us -> 36.6 us (0.82)
  local copies, waits for them, and re-layouts: 8.06 us -> 0 us
    unnamed x22 -> x0, local copies, waits for them, and re-layouts: 8.06 us -> none
where the time goes in v3:
time: 36.6 us; the launch traced here: 36.4 us
  Pallas kernels  35.8 us (98%)
  between operations  0.64 us (2%)
    pallas_call x1, Pallas kernels, body(): pl.pallas_call(functools.partial(kernel, n, cells, chunk), out_shape=(jax...  33.7 us
    pallas_call x1, Pallas kernels, body(): pl.pallas_call(unpack, out_shape=(jax.ShapeDtypeStruct((4, rows, cols, de...  2.05 us

profile of v3, /device:TPU:0, one launch (start us, length us, event | category | flops | bytes accessed | tf_op | source)
XLA Modules:
  0.0 36.4 jit_solution(3064533747084628447)
XLA Ops:
  0.6 33.7 %shard_map.111 = (bf16[4,2,8,128]{3,2,1,0:T(8,128)(2,1)}, bf16[2,512,128]{2,1,0:T(8,128)(2,1)}) custom-call(bf16[3,2,8,128]{3,2,1,0:T(8,128)(2,1)} %refs_0_.1, bf16[3,27,64]{2,1,0:T(8,128)(2,1)} %bitcast.2, bf16[27,64,64]{2,1,0:T(8,128)(2,1)} %refs_2_.1, bf16[27,4,64]{2,1,0:T(4,128)(2,1)} %refs_3_.1, f32[3,2,8,128]{3,2,1,0:T(8,128)} %refs_4_.1, ...), custom_call_target="tpu_custom_call" | custom-call | tf_op jit(solution)/shard_map/pallas_call | solution.py:533
  34.3 2.1 %shard_map.112 = (bf16[4,2,8,128]{3,2,1,0:T(8,128)(2,1)}, f32[3,27,64]{2,1,0:T(8,128)}, f32[27,64,64]{2,1,0:T(8,128)}, f32[27,4,64]{2,1,0:T(4,128)}) custom-call(bf16[4,2,8,128]{3,2,1,0:T(8,128)(2,1)} %get-tuple-element.10.pred_in, bf16[2,512,128]{2,1,0:T(8,128)(2,1)} %get-tuple-element.11.gat_hbm), custom_call_target="tpu_custom_call" | custom-call | tf_op jit(solution)/shard_map/pallas_call | solution.py:546
